TPU v7x, 256 devices: a whole 4x4x8 slice. The times are simulated.
256 devices in a mesh: seq: 32 (over x, z), head: 8 (over y, core).
Axes of the slice: x: 4, y: 4, z: 8, core: 2. Of those that a mesh axis runs over, the one named last changes fastest.
Arguments:
- projected: bfloat16 [3, 16384, 4096], P(None, 'seq', 'head'), may hold values from -6 to 6
- conv_weight: float32 [3, 4, 4096], P(None, None, 'head'), may hold values from -3 to 3
- out_weight: bfloat16 [4096, 4096], P('head'), may hold values from -0.09375 to 0.09375
- out_grad: bfloat16 [16384, 4096], P('seq', 'head'), may hold values from -6 to 6
- doc_lengths: int32 [8], replicated, may hold values from 1 to 4096, 16384 in all
Outputs:
- mixed: bfloat16 [16384, 4096], P('seq', 'head')
- grad_projected: bfloat16 [3, 16384, 4096], P(None, 'seq', 'head')
- grad_conv: float32 [3, 4, 4096], P(None, None, 'head')
- grad_out_weight: float32 [4096, 4096], P('head', 'seq')
Inputs may be any that keep to these rules, and one draw needn't show every extreme that they name: `doc_lengths`: the lengths sum to 16384 and the longest is exactly 4096.
All inputs are finite; a program needn't handle non-finite values.
Results may differ from a plain program's by a relative error of at most 0.017.
Values may be sent and summed in bfloat16 or wider, within the bound.
A program may use at most 128 MiB of HBM per device.

v0:
```python
import jax
import jax.numpy as jnp
from jax import lax
from jax.sharding import PartitionSpec as P

DH = 128
KW = 4


def from_behind(array, axis, by):
    peers = lax.axis_size(axis)
    pairs = [(i, i + by) for i in range(peers) if 0 <= i + by < peers]
    return lax.ppermute(array, axis, pairs)


def segment_of(doc_starts, positions):
    counted = jnp.sum((doc_starts[None, :] <= positions[:, None]).astype(jnp.int32), axis=1)
    return counted - 1


def pass_along(resets, local, length, moving):

    def advance(number, incoming):
        return moving(local + (1.0 - resets) * incoming)

    return lax.fori_loop(0, length, advance, jnp.zeros_like(local))


def carry_forward(resets, local):
    return pass_along(
        resets, local, lax.axis_size("seq") - 1, lambda moving: from_behind(moving, "seq", 1)
    )


def carry_backward(resets, local):
    return pass_along(
        resets, local, lax.axis_size("seq") - 1, lambda moving: from_behind(moving, "seq", -1)
    )


def feature_map(field):
    return jax.nn.elu(field) + 1.0


def feature_slope(field):
    return jnp.where(field > 0, 1.0, jnp.exp(jnp.minimum(field, 0.0)))


def body(projected, conv_weight, out_weight, out_grad, doc_lengths):
    tok_rows = projected.shape[1]
    channels = projected.shape[2]
    head_count = channels // DH
    high = lax.Precision.HIGHEST
    offset = lax.axis_index("seq") * tok_rows
    doc_starts = jnp.cumsum(doc_lengths) - doc_lengths
    positions = offset + jnp.arange(-(KW - 1), tok_rows + KW - 1, dtype=jnp.int32)
    doc_all = segment_of(doc_starts, positions)
    doc_here = doc_all[KW - 1 : KW - 1 + tok_rows]
    doc_before = doc_all[KW - 2]
    doc_last = doc_all[KW - 2 + tok_rows]
    rim = from_behind(projected[:, tok_rows - (KW - 1) :, :], "seq", 1)
    extended = jnp.concatenate([rim, projected], axis=1)
    conv_sum = jnp.zeros((3, tok_rows, channels), jnp.float32)
    masks = []
    for tap in range(KW):
        kept = (doc_all[KW - 1 - tap : KW - 1 - tap + tok_rows] == doc_here).astype(jnp.float32)
        masks.append(kept)
        conv_sum = (
            conv_sum
            + conv_weight[:, tap, None, :]
            * extended[:, KW - 1 - tap : KW - 1 - tap + tok_rows, :]
            * kept[None, :, None]
        )
    acts = conv_sum.astype(jnp.bfloat16)
    query_raw = acts[0].reshape(tok_rows, head_count, DH).astype(jnp.float32)
    key_raw = acts[1].reshape(tok_rows, head_count, DH).astype(jnp.float32)
    value_float = acts[2].reshape(tok_rows, head_count, DH).astype(jnp.float32)
    query_float = feature_map(query_raw)
    key_float = feature_map(key_raw)
    places = jnp.arange(tok_rows)
    allowed = (places[None, :] <= places[:, None]) & (doc_here[:, None] == doc_here[None, :])
    scores = jnp.einsum("thd,shd->hts", query_float, key_float, precision=high)
    weights = jnp.where(allowed[None], scores, 0.0)
    local_out = jnp.einsum("hts,shd->thd", weights, value_float, precision=high)
    head_mask = (doc_here == doc_before).astype(jnp.float32)[:, None, None]
    tail_keep = doc_here == doc_last
    tail_mask = tail_keep.astype(jnp.float32)[:, None, None]
    resets = (doc_last != doc_before).astype(jnp.float32)
    tail_state = jnp.einsum("thd,the->hde", key_float * tail_mask, value_float, precision=high)
    state_in = carry_forward(resets, tail_state)
    outputs = local_out + head_mask * jnp.einsum(
        "thd,hde->the", query_float, state_in, precision=high
    )
    scale = lax.rsqrt(jnp.mean(outputs * outputs, axis=-1, keepdims=True) + 1e-06)
    unit = outputs * scale
    normed = unit.reshape(tok_rows, channels).astype(jnp.bfloat16)
    columns = out_weight
    summed = lax.psum_scatter(
        lax.dot_general(
            columns, normed, (((0,), (1,)), ((), ())), preferred_element_type=jnp.float32
        ).astype(jnp.bfloat16),
        "head",
        scatter_dimension=0,
        tiled=True,
    ).astype(jnp.float32)
    mixed = summed.T.astype(jnp.bfloat16)
    full_grad = lax.all_gather(out_grad, "head", axis=1, tiled=True)
    columns = full_grad
    grad_out_weight = lax.psum_scatter(
        lax.dot_general(
            columns, normed, (((0,), (0,)), ((), ())), preferred_element_type=jnp.float32
        ),
        "seq",
        scatter_dimension=0,
        tiled=True,
    ).T
    grad_unit = lax.dot_general(
        full_grad, out_weight, (((1,), (1,)), ((), ())), preferred_element_type=jnp.float32
    )
    grad_unit = grad_unit.reshape(tok_rows, head_count, DH)
    grad_outputs = scale * (grad_unit - unit * jnp.mean(grad_unit * unit, axis=-1, keepdims=True))
    grad_weights = jnp.where(
        allowed[None], jnp.einsum("thd,shd->hts", grad_outputs, value_float, precision=high), 0.0
    )
    grad_back = jnp.einsum("thd,the->hde", query_float * head_mask, grad_outputs, precision=high)
    state_out = carry_backward(resets, grad_back)
    grad_query = jnp.einsum("hts,shd->thd", grad_weights, key_float, precision=high)
    grad_query = grad_query + head_mask * jnp.einsum(
        "the,hde->thd", grad_outputs, state_in, precision=high
    )
    grad_query = grad_query * feature_slope(query_raw)
    grad_key = jnp.einsum("hts,thd->shd", grad_weights, query_float, precision=high)
    grad_key = grad_key + tail_mask * jnp.einsum(
        "hde,she->shd", state_out, value_float, precision=high
    )
    grad_key = grad_key * feature_slope(key_raw)
    grad_value = jnp.einsum("hts,thd->shd", weights, grad_outputs, precision=high)
    grad_value = grad_value + tail_mask * jnp.einsum(
        "shd,hde->she", key_float, state_out, precision=high
    )
    grad_acts = jnp.stack([grad_query, grad_key, grad_value], axis=0).reshape(3, tok_rows, channels)
    ahead = from_behind(grad_acts[:, : KW - 1, :], "seq", -1)
    grad_ext = jnp.concatenate([grad_acts, ahead], axis=1)
    grad_raw = jnp.zeros((3, tok_rows, channels), jnp.float32)
    tap_sums = []
    for tap in range(KW):
        kept_next = (doc_all[KW - 1 + tap : KW - 1 + tap + tok_rows] == doc_here).astype(
            jnp.float32
        )
        grad_raw = (
            grad_raw
            + conv_weight[:, tap, None, :]
            * grad_ext[:, tap : tap + tok_rows, :]
            * kept_next[None, :, None]
        )
        lagged_raw = extended[:, KW - 1 - tap : KW - 1 - tap + tok_rows, :]
        tap_sums.append(jnp.sum(grad_acts * lagged_raw * masks[tap][None, :, None], axis=1))
    grad_conv = lax.psum(jnp.stack(tap_sums, axis=1), "seq")
    return (mixed, grad_raw.astype(jnp.bfloat16), grad_conv, grad_out_weight)


def solution(mesh):
    return jax.shard_map(
        body,
        mesh=mesh,
        in_specs=(
            P(None, "seq", "head"),
            P(None, None, "head"),
            P("head", None),
            P("seq", "head"),
            P(),
        ),
        out_specs=(
            P("seq", "head"),
            P(None, "seq", "head"),
            P(None, None, "head"),
            P("head", "seq"),
        ),
        check_vma=False,
    )
```

profile of v0, /device:TPU:6, one launch (start us, length us, event | category | flops | bytes accessed | tf_op | source)
XLA Modules:
  0.0 1010.8 jit_solution(12537721194010584494)
XLA Ops:
  30.3 349.2 %while.24 = (s32[]{:T(128)}, f32[4,128,128]{2,1,0:T(8,128)S(1)}, f32[]{:T(128)}, f32[4,128,128]{2,1,0:T(8,128)S(1)}, s32[]{:T(128)}) while((s32[]{:T(128)}, f32[4,128,128]{2,1,0:T(8,128)S(1)}, f32[]{:T(128)}, f32[4,128,128]{2,1,0:T(8,128)S(1)}, s32[]{:T(128)}) %tuple.73), condition=%wide.region_3.4_spmd, body=%wide.region_2.3_spmd.sunk | while | flops 131074 | bytes 1835113 | solution.py:26
  34.1 8.6 collective-permute-done
  44.7 9.6 collective-permute-done
  56.2 8.6 collective-permute-done
  66.8 8.4 collective-permute-done
  77.2 8.4 collective-permute-done
  87.6 8.4 collective-permute-done
  98.0 8.9 collective-permute-done
  108.9 10.0 collective-permute-done
  120.9 11.2 %collective-permute-done = f32[4,128,128]{2,1,0:T(8,128)S(1)} collective-permute-done((f32[4,128,128]{2,1,0:T(8,128)S(1)}, f32[4,128,128]{2,1,0:T(8,128)S(1)}, u32[]{:S(2)}, u32[]{:S(2)}) %collective-permute-start) | collective-permute-done | bytes 262176 | tf_op jit(solution)/shard_map/while/body/eval_jaxpr/ppermute | solution.py:13
  134.1 10.4 %collective-permute-done = f32[4,128,128]{2,1,0:T(8,128)S(1)} collective-permute-done((f32[4,128,128]{2,1,0:T(8,128)S(1)}, f32[4,128,128]{2,1,0:T(8,128)S(1)}, u32[]{:S(2)}, u32[]{:S(2)}) %collective-permute-start) | collective-permute-done | bytes 262176 | tf_op jit(solution)/shard_map/while/body/eval_jaxpr/ppermute | solution.py:13
  146.4 9.6 collective-permute-done
  157.9 8.6 collective-permute-done
  168.6 8.4 collective-permute-done
  179.0 8.4 collective-permute-done
  189.4 8.4 collective-permute-done
  199.8 8.9 collective-permute-done
  210.7 10.0 collective-permute-done
  222.6 11.2 %collective-permute-done = f32[4,128,128]{2,1,0:T(8,128)S(1)} collective-permute-done((f32[4,128,128]{2,1,0:T(8,128)S(1)}, f32[4,128,128]{2,1,0:T(8,128)S(1)}, u32[]{:S(2)}, u32[]{:S(2)}) %collective-permute-start) | collective-permute-done | bytes 262176 | tf_op jit(solution)/shard_map/while/body/eval_jaxpr/ppermute | solution.py:13
  235.8 10.4 %collective-permute-done = f32[4,128,128]{2,1,0:T(8,128)S(1)} collective-permute-done((f32[4,128,128]{2,1,0:T(8,128)S(1)}, f32[4,128,128]{2,1,0:T(8,128)S(1)}, u32[]{:S(2)}, u32[]{:S(2)}) %collective-permute-start) | collective-permute-done | bytes 262176 | tf_op jit(solution)/shard_map/while/body/eval_jaxpr/ppermute | solution.py:13
  248.1 9.6 collective-permute-done
  259.7 8.6 collective-permute-done
  270.3 8.4 collective-permute-done
  280.7 8.4 collective-permute-done
  291.1 8.4 collective-permute-done
  301.5 8.9 collective-permute-done
  312.4 10.0 collective-permute-done
  324.4 11.2 %collective-permute-done = f32[4,128,128]{2,1,0:T(8,128)S(1)} collective-permute-done((f32[4,128,128]{2,1,0:T(8,128)S(1)}, f32[4,128,128]{2,1,0:T(8,128)S(1)}, u32[]{:S(2)}, u32[]{:S(2)}) %collective-permute-start) | collective-permute-done | bytes 262176 | tf_op jit(solution)/shard_map/while/body/eval_jaxpr/ppermute | solution.py:13
  337.5 10.4 %collective-permute-done = f32[4,128,128]{2,1,0:T(8,128)S(1)} collective-permute-done((f32[4,128,128]{2,1,0:T(8,128)S(1)}, f32[4,128,128]{2,1,0:T(8,128)S(1)}, u32[]{:S(2)}, u32[]{:S(2)}) %collective-permute-start) | collective-permute-done | bytes 262176 | tf_op jit(solution)/shard_map/while/body/eval_jaxpr/ppermute | solution.py:13
  349.9 8.4 collective-permute-done
  360.3 8.4 collective-permute-done
  370.7 8.4 collective-permute-done
  396.4 15.7 %fusion = bf16[4096,512]{0,1:T(8,128)(2,1)} fusion(bf16[512,512]{0,1:T(8,128)(2,1)S(1)} %bitcast.81, bf16[512,4096]{1,0:T(8,128)(2,1)S(1)} %copy-done.2), kind=kOutput, calls=%fused_computation.4 | convolution fusion | flops 2149580800 | bytes 8912896 | tf_op jit(solution)/shard_map/dot_general | solution.py:99
  412.2 7.9 convolution_bitcast_fusion
  422.4 414.1 %while.25 = (s32[]{:T(128)}, f32[4,128,128]{2,1,0:T(8,128)S(1)}, f32[]{:T(128)}, f32[4,128,128]{2,1,0:T(8,128)}, s32[]{:T(128)}) while((s32[]{:T(128)}, f32[4,128,128]{2,1,0:T(8,128)S(1)}, f32[]{:T(128)}, f32[4,128,128]{2,1,0:T(8,128)}, s32[]{:T(128)}) %tuple.76), condition=%wide.region_8.9_spmd, body=%wide.region_7.8_spmd.sunk | while | flops 131074 | bytes 1835113 | solution.py:26
  426.1 6.5 collective-permute-done.1
  440.5 6.5 collective-permute-done.1
  462.4 6.4 collective-permute-start.1
  468.8 8.1 collective-permute-done.1
  478.6 6.4 collective-permute-start.1
  485.0 6.6 collective-permute-done.1
  493.3 6.4 collective-permute-start.1
  506.8 6.4 collective-permute-start.1
  534.3 6.5 collective-permute-start.1
  548.3 6.4 collective-permute-start.1
  561.1 6.4 collective-permute-start.1
  586.9 6.5 collective-permute-start.1
  601.0 6.4 collective-permute-start.1
  607.5 6.9 collective-permute-done.1
  616.1 6.4 collective-permute-start.1
  630.2 6.4 collective-permute-start.1
  643.4 6.5 collective-permute-start.1
  655.7 6.4 collective-permute-start.1
  668.0 6.4 collective-permute-start.1
  681.2 6.5 collective-permute-start.1
  687.7 6.7 collective-permute-done.1
  720.9 6.4 collective-permute-start.1
  734.5 6.4 collective-permute-start.1
  740.9 6.7 collective-permute-done.1
  749.3 6.4 collective-permute-start.1
  763.5 6.4 collective-permute-start.1
  859.0 8.3 fusion.55
  875.3 6.4 collective-permute-start.3
  881.7 118.3 %psum.7 = f32[3,4,512]{2,0,1:T(4,128)S(1)} all-reduce(f32[3,4,512]{2,0,1:T(4,128)S(1)} %pad_maximum_fusion.3), channel_id=1, replica_groups=mesh['seq'=32,'head'=8] {'seq'}, use_global_device_ids=true, to_apply=%region_13.14 | all-reduce | flops 6144 | bytes 49152 | tf_op jit(solution)/shard_map/psum | solution.py:158
  (211 shorter events, 381.3 us)
Async XLA Ops:
  7.2 381.9 %all-gather.2.cloned.1.call-start = ((), (), s32[]{:S(2)}) async-start(), calls=%async_computation.3 | async-start | bytes 4718592 | tf_op jit(solution)/shard_map/all_gather | solution.py:107
  7.9 996.2 %reduce-scatter.3.cloned.1.call-start = ((), (), s32[]{:S(2)}) async-start(), calls=%async_computation.2 | async-start | bytes 4718592 | tf_op jit(solution)/shard_map/reduce_scatter | solution.py:98
  8.7 10.6 %collective-permute-start.2 = (bf16[3,3,512]{2,1,0:T(4,128)(2,1)S(1)}, bf16[3,3,512]{2,1,0:T(4,128)(2,1)S(1)}, u32[]{:S(2)}, u32[]{:S(2)}) collective-permute-start(bf16[3,3,512]{2,1,0:T(4,128)(2,1)S(1)} %slice.83), channel_id=1, source_target_pairs={{0,8},{8,16},{16,24},{24,32},{32,40},{40,48},{48,56},{56,64},{64,7... | collective-permute-start | bytes 27656 | tf_op jit(solution)/shard_map/ppermute | solution.py:13
  30.3 12.4 %collective-permute-start = (f32[4,128,128]{2,1,0:T(8,128)S(1)}, f32[4,128,128]{2,1,0:T(8,128)S(1)}, u32[]{:S(2)}, u32[]{:S(2)}) collective-permute-start(f32[4,128,128]{2,1,0:T(8,128)S(1)} %multiply_add_fusion.4), channel_id=1, source_target_pairs={{0,8},{8,16},{16,24},{24,32},{32,40},{40,48},{48,56},{56,64},{64,7... | collective-permute-start | bytes 786440 | tf_op jit(solution)/shard_map/while/body/eval_jaxpr/ppermute | solution.py:13
  42.8 11.5 %collective-permute-start = (f32[4,128,128]{2,1,0:T(8,128)S(1)}, f32[4,128,128]{2,1,0:T(8,128)S(1)}, u32[]{:S(2)}, u32[]{:S(2)}) collective-permute-start(f32[4,128,128]{2,1,0:T(8,128)S(1)} %multiply_add_fusion.4), channel_id=1, source_target_pairs={{0,8},{8,16},{16,24},{24,32},{32,40},{40,48},{48,56},{56,64},{64,7... | collective-permute-start | bytes 786440 | tf_op jit(solution)/shard_map/while/body/eval_jaxpr/ppermute | solution.py:13
  54.3 10.6 %collective-permute-start = (f32[4,128,128]{2,1,0:T(8,128)S(1)}, f32[4,128,128]{2,1,0:T(8,128)S(1)}, u32[]{:S(2)}, u32[]{:S(2)}) collective-permute-start(f32[4,128,128]{2,1,0:T(8,128)S(1)} %multiply_add_fusion.4), channel_id=1, source_target_pairs={{0,8},{8,16},{16,24},{24,32},{32,40},{40,48},{48,56},{56,64},{64,7... | collective-permute-start | bytes 786440 | tf_op jit(solution)/shard_map/while/body/eval_jaxpr/ppermute | solution.py:13
  64.9 10.4 %collective-permute-start = (f32[4,128,128]{2,1,0:T(8,128)S(1)}, f32[4,128,128]{2,1,0:T(8,128)S(1)}, u32[]{:S(2)}, u32[]{:S(2)}) collective-permute-start(f32[4,128,128]{2,1,0:T(8,128)S(1)} %multiply_add_fusion.4), channel_id=1, source_target_pairs={{0,8},{8,16},{16,24},{24,32},{32,40},{40,48},{48,56},{56,64},{64,7... | collective-permute-start | bytes 786440 | tf_op jit(solution)/shard_map/while/body/eval_jaxpr/ppermute | solution.py:13
  75.3 10.4 %collective-permute-start = (f32[4,128,128]{2,1,0:T(8,128)S(1)}, f32[4,128,128]{2,1,0:T(8,128)S(1)}, u32[]{:S(2)}, u32[]{:S(2)}) collective-permute-start(f32[4,128,128]{2,1,0:T(8,128)S(1)} %multiply_add_fusion.4), channel_id=1, source_target_pairs={{0,8},{8,16},{16,24},{24,32},{32,40},{40,48},{48,56},{56,64},{64,7... | collective-permute-start | bytes 786440 | tf_op jit(solution)/shard_map/while/body/eval_jaxpr/ppermute | solution.py:13
  85.7 10.4 %collective-permute-start = (f32[4,128,128]{2,1,0:T(8,128)S(1)}, f32[4,128,128]{2,1,0:T(8,128)S(1)}, u32[]{:S(2)}, u32[]{:S(2)}) collective-permute-start(f32[4,128,128]{2,1,0:T(8,128)S(1)} %multiply_add_fusion.4), channel_id=1, source_target_pairs={{0,8},{8,16},{16,24},{24,32},{32,40},{40,48},{48,56},{56,64},{64,7... | collective-permute-start | bytes 786440 | tf_op jit(solution)/shard_map/while/body/eval_jaxpr/ppermute | solution.py:13
  96.1 10.8 %collective-permute-start = (f32[4,128,128]{2,1,0:T(8,128)S(1)}, f32[4,128,128]{2,1,0:T(8,128)S(1)}, u32[]{:S(2)}, u32[]{:S(2)}) collective-permute-start(f32[4,128,128]{2,1,0:T(8,128)S(1)} %multiply_add_fusion.4), channel_id=1, source_target_pairs={{0,8},{8,16},{16,24},{24,32},{32,40},{40,48},{48,56},{56,64},{64,7... | collective-permute-start | bytes 786440 | tf_op jit(solution)/shard_map/while/body/eval_jaxpr/ppermute | solution.py:13
  107.0 12.0 %collective-permute-start = (f32[4,128,128]{2,1,0:T(8,128)S(1)}, f32[4,128,128]{2,1,0:T(8,128)S(1)}, u32[]{:S(2)}, u32[]{:S(2)}) collective-permute-start(f32[4,128,128]{2,1,0:T(8,128)S(1)} %multiply_add_fusion.4), channel_id=1, source_target_pairs={{0,8},{8,16},{16,24},{24,32},{32,40},{40,48},{48,56},{56,64},{64,7... | collective-permute-start | bytes 786440 | tf_op jit(solution)/shard_map/while/body/eval_jaxpr/ppermute | solution.py:13
  119.0 13.1 %collective-permute-start = (f32[4,128,128]{2,1,0:T(8,128)S(1)}, f32[4,128,128]{2,1,0:T(8,128)S(1)}, u32[]{:S(2)}, u32[]{:S(2)}) collective-permute-start(f32[4,128,128]{2,1,0:T(8,128)S(1)} %multiply_add_fusion.4), channel_id=1, source_target_pairs={{0,8},{8,16},{16,24},{24,32},{32,40},{40,48},{48,56},{56,64},{64,7... | collective-permute-start | bytes 786440 | tf_op jit(solution)/shard_map/while/body/eval_jaxpr/ppermute | solution.py:13
  132.1 12.3 %collective-permute-start = (f32[4,128,128]{2,1,0:T(8,128)S(1)}, f32[4,128,128]{2,1,0:T(8,128)S(1)}, u32[]{:S(2)}, u32[]{:S(2)}) collective-permute-start(f32[4,128,128]{2,1,0:T(8,128)S(1)} %multiply_add_fusion.4), channel_id=1, source_target_pairs={{0,8},{8,16},{16,24},{24,32},{32,40},{40,48},{48,56},{56,64},{64,7... | collective-permute-start | bytes 786440 | tf_op jit(solution)/shard_map/while/body/eval_jaxpr/ppermute | solution.py:13
  144.5 11.5 %collective-permute-start = (f32[4,128,128]{2,1,0:T(8,128)S(1)}, f32[4,128,128]{2,1,0:T(8,128)S(1)}, u32[]{:S(2)}, u32[]{:S(2)}) collective-permute-start(f32[4,128,128]{2,1,0:T(8,128)S(1)} %multiply_add_fusion.4), channel_id=1, source_target_pairs={{0,8},{8,16},{16,24},{24,32},{32,40},{40,48},{48,56},{56,64},{64,7... | collective-permute-start | bytes 786440 | tf_op jit(solution)/shard_map/while/body/eval_jaxpr/ppermute | solution.py:13
  156.0 10.6 %collective-permute-start = (f32[4,128,128]{2,1,0:T(8,128)S(1)}, f32[4,128,128]{2,1,0:T(8,128)S(1)}, u32[]{:S(2)}, u32[]{:S(2)}) collective-permute-start(f32[4,128,128]{2,1,0:T(8,128)S(1)} %multiply_add_fusion.4), channel_id=1, source_target_pairs={{0,8},{8,16},{16,24},{24,32},{32,40},{40,48},{48,56},{56,64},{64,7... | collective-permute-start | bytes 786440 | tf_op jit(solution)/shard_map/while/body/eval_jaxpr/ppermute | solution.py:13
  166.6 10.4 %collective-permute-start = (f32[4,128,128]{2,1,0:T(8,128)S(1)}, f32[4,128,128]{2,1,0:T(8,128)S(1)}, u32[]{:S(2)}, u32[]{:S(2)}) collective-permute-start(f32[4,128,128]{2,1,0:T(8,128)S(1)} %multiply_add_fusion.4), channel_id=1, source_target_pairs={{0,8},{8,16},{16,24},{24,32},{32,40},{40,48},{48,56},{56,64},{64,7... | collective-permute-start | bytes 786440 | tf_op jit(solution)/shard_map/while/body/eval_jaxpr/ppermute | solution.py:13
  177.0 10.4 %collective-permute-start = (f32[4,128,128]{2,1,0:T(8,128)S(1)}, f32[4,128,128]{2,1,0:T(8,128)S(1)}, u32[]{:S(2)}, u32[]{:S(2)}) collective-permute-start(f32[4,128,128]{2,1,0:T(8,128)S(1)} %multiply_add_fusion.4), channel_id=1, source_target_pairs={{0,8},{8,16},{16,24},{24,32},{32,40},{40,48},{48,56},{56,64},{64,7... | collective-permute-start | bytes 786440 | tf_op jit(solution)/shard_map/while/body/eval_jaxpr/ppermute | solution.py:13
  187.4 10.4 %collective-permute-start = (f32[4,128,128]{2,1,0:T(8,128)S(1)}, f32[4,128,128]{2,1,0:T(8,128)S(1)}, u32[]{:S(2)}, u32[]{:S(2)}) collective-permute-start(f32[4,128,128]{2,1,0:T(8,128)S(1)} %multiply_add_fusion.4), channel_id=1, source_target_pairs={{0,8},{8,16},{16,24},{24,32},{32,40},{40,48},{48,56},{56,64},{64,7... | collective-permute-start | bytes 786440 | tf_op jit(solution)/shard_map/while/body/eval_jaxpr/ppermute | solution.py:13
  197.8 10.8 %collective-permute-start = (f32[4,128,128]{2,1,0:T(8,128)S(1)}, f32[4,128,128]{2,1,0:T(8,128)S(1)}, u32[]{:S(2)}, u32[]{:S(2)}) collective-permute-start(f32[4,128,128]{2,1,0:T(8,128)S(1)} %multiply_add_fusion.4), channel_id=1, source_target_pairs={{0,8},{8,16},{16,24},{24,32},{32,40},{40,48},{48,56},{56,64},{64,7... | collective-permute-start | bytes 786440 | tf_op jit(solution)/shard_map/while/body/eval_jaxpr/ppermute | solution.py:13
  208.7 12.0 %collective-permute-start = (f32[4,128,128]{2,1,0:T(8,128)S(1)}, f32[4,128,128]{2,1,0:T(8,128)S(1)}, u32[]{:S(2)}, u32[]{:S(2)}) collective-permute-start(f32[4,128,128]{2,1,0:T(8,128)S(1)} %multiply_add_fusion.4), channel_id=1, source_target_pairs={{0,8},{8,16},{16,24},{24,32},{32,40},{40,48},{48,56},{56,64},{64,7... | collective-permute-start | bytes 786440 | tf_op jit(solution)/shard_map/while/body/eval_jaxpr/ppermute | solution.py:13
  220.7 13.1 %collective-permute-start = (f32[4,128,128]{2,1,0:T(8,128)S(1)}, f32[4,128,128]{2,1,0:T(8,128)S(1)}, u32[]{:S(2)}, u32[]{:S(2)}) collective-permute-start(f32[4,128,128]{2,1,0:T(8,128)S(1)} %multiply_add_fusion.4), channel_id=1, source_target_pairs={{0,8},{8,16},{16,24},{24,32},{32,40},{40,48},{48,56},{56,64},{64,7... | collective-permute-start | bytes 786440 | tf_op jit(solution)/shard_map/while/body/eval_jaxpr/ppermute | solution.py:13
  233.8 12.3 %collective-permute-start = (f32[4,128,128]{2,1,0:T(8,128)S(1)}, f32[4,128,128]{2,1,0:T(8,128)S(1)}, u32[]{:S(2)}, u32[]{:S(2)}) collective-permute-start(f32[4,128,128]{2,1,0:T(8,128)S(1)} %multiply_add_fusion.4), channel_id=1, source_target_pairs={{0,8},{8,16},{16,24},{24,32},{32,40},{40,48},{48,56},{56,64},{64,7... | collective-permute-start | bytes 786440 | tf_op jit(solution)/shard_map/while/body/eval_jaxpr/ppermute | solution.py:13
  246.2 11.5 %collective-permute-start = (f32[4,128,128]{2,1,0:T(8,128)S(1)}, f32[4,128,128]{2,1,0:T(8,128)S(1)}, u32[]{:S(2)}, u32[]{:S(2)}) collective-permute-start(f32[4,128,128]{2,1,0:T(8,128)S(1)} %multiply_add_fusion.4), channel_id=1, source_target_pairs={{0,8},{8,16},{16,24},{24,32},{32,40},{40,48},{48,56},{56,64},{64,7... | collective-permute-start | bytes 786440 | tf_op jit(solution)/shard_map/while/body/eval_jaxpr/ppermute | solution.py:13
  257.7 10.6 %collective-permute-start = (f32[4,128,128]{2,1,0:T(8,128)S(1)}, f32[4,128,128]{2,1,0:T(8,128)S(1)}, u32[]{:S(2)}, u32[]{:S(2)}) collective-permute-start(f32[4,128,128]{2,1,0:T(8,128)S(1)} %multiply_add_fusion.4), channel_id=1, source_target_pairs={{0,8},{8,16},{16,24},{24,32},{32,40},{40,48},{48,56},{56,64},{64,7... | collective-permute-start | bytes 786440 | tf_op jit(solution)/shard_map/while/body/eval_jaxpr/ppermute | solution.py:13
  268.3 10.4 %collective-permute-start = (f32[4,128,128]{2,1,0:T(8,128)S(1)}, f32[4,128,128]{2,1,0:T(8,128)S(1)}, u32[]{:S(2)}, u32[]{:S(2)}) collective-permute-start(f32[4,128,128]{2,1,0:T(8,128)S(1)} %multiply_add_fusion.4), channel_id=1, source_target_pairs={{0,8},{8,16},{16,24},{24,32},{32,40},{40,48},{48,56},{56,64},{64,7... | collective-permute-start | bytes 786440 | tf_op jit(solution)/shard_map/while/body/eval_jaxpr/ppermute | solution.py:13
  278.7 10.4 %collective-permute-start = (f32[4,128,128]{2,1,0:T(8,128)S(1)}, f32[4,128,128]{2,1,0:T(8,128)S(1)}, u32[]{:S(2)}, u32[]{:S(2)}) collective-permute-start(f32[4,128,128]{2,1,0:T(8,128)S(1)} %multiply_add_fusion.4), channel_id=1, source_target_pairs={{0,8},{8,16},{16,24},{24,32},{32,40},{40,48},{48,56},{56,64},{64,7... | collective-permute-start | bytes 786440 | tf_op jit(solution)/shard_map/while/body/eval_jaxpr/ppermute | solution.py:13
  289.2 10.4 %collective-permute-start = (f32[4,128,128]{2,1,0:T(8,128)S(1)}, f32[4,128,128]{2,1,0:T(8,128)S(1)}, u32[]{:S(2)}, u32[]{:S(2)}) collective-permute-start(f32[4,128,128]{2,1,0:T(8,128)S(1)} %multiply_add_fusion.4), channel_id=1, source_target_pairs={{0,8},{8,16},{16,24},{24,32},{32,40},{40,48},{48,56},{56,64},{64,7... | collective-permute-start | bytes 786440 | tf_op jit(solution)/shard_map/while/body/eval_jaxpr/ppermute | solution.py:13
  299.6 10.8 %collective-permute-start = (f32[4,128,128]{2,1,0:T(8,128)S(1)}, f32[4,128,128]{2,1,0:T(8,128)S(1)}, u32[]{:S(2)}, u32[]{:S(2)}) collective-permute-start(f32[4,128,128]{2,1,0:T(8,128)S(1)} %multiply_add_fusion.4), channel_id=1, source_target_pairs={{0,8},{8,16},{16,24},{24,32},{32,40},{40,48},{48,56},{56,64},{64,7... | collective-permute-start | bytes 786440 | tf_op jit(solution)/shard_map/while/body/eval_jaxpr/ppermute | solution.py:13
  310.4 12.0 %collective-permute-start = (f32[4,128,128]{2,1,0:T(8,128)S(1)}, f32[4,128,128]{2,1,0:T(8,128)S(1)}, u32[]{:S(2)}, u32[]{:S(2)}) collective-permute-start(f32[4,128,128]{2,1,0:T(8,128)S(1)} %multiply_add_fusion.4), channel_id=1, source_target_pairs={{0,8},{8,16},{16,24},{24,32},{32,40},{40,48},{48,56},{56,64},{64,7... | collective-permute-start | bytes 786440 | tf_op jit(solution)/shard_map/while/body/eval_jaxpr/ppermute | solution.py:13
  322.4 13.1 %collective-permute-start = (f32[4,128,128]{2,1,0:T(8,128)S(1)}, f32[4,128,128]{2,1,0:T(8,128)S(1)}, u32[]{:S(2)}, u32[]{:S(2)}) collective-permute-start(f32[4,128,128]{2,1,0:T(8,128)S(1)} %multiply_add_fusion.4), channel_id=1, source_target_pairs={{0,8},{8,16},{16,24},{24,32},{32,40},{40,48},{48,56},{56,64},{64,7... | collective-permute-start | bytes 786440 | tf_op jit(solution)/shard_map/while/body/eval_jaxpr/ppermute | solution.py:13
  335.6 12.3 %collective-permute-start = (f32[4,128,128]{2,1,0:T(8,128)S(1)}, f32[4,128,128]{2,1,0:T(8,128)S(1)}, u32[]{:S(2)}, u32[]{:S(2)}) collective-permute-start(f32[4,128,128]{2,1,0:T(8,128)S(1)} %multiply_add_fusion.4), channel_id=1, source_target_pairs={{0,8},{8,16},{16,24},{24,32},{32,40},{40,48},{48,56},{56,64},{64,7... | collective-permute-start | bytes 786440 | tf_op jit(solution)/shard_map/while/body/eval_jaxpr/ppermute | solution.py:13
  347.9 10.4 %collective-permute-start = (f32[4,128,128]{2,1,0:T(8,128)S(1)}, f32[4,128,128]{2,1,0:T(8,128)S(1)}, u32[]{:S(2)}, u32[]{:S(2)}) collective-permute-start(f32[4,128,128]{2,1,0:T(8,128)S(1)} %multiply_add_fusion.4), channel_id=1, source_target_pairs={{0,8},{8,16},{16,24},{24,32},{32,40},{40,48},{48,56},{56,64},{64,7... | collective-permute-start | bytes 786440 | tf_op jit(solution)/shard_map/while/body/eval_jaxpr/ppermute | solution.py:13
  412.2 591.9 %reduce-scatter.5.cloned.1.call-start = ((), (), s32[]{:S(2)}) async-start(), calls=%async_computation.4 | async-start | bytes 8650752 | tf_op jit(solution)/shard_map/reduce_scatter | solution.py:109
  434.3 12.7 %collective-permute-start.1 = (f32[4,128,128]{2,1,0:T(8,128)}, f32[4,128,128]{2,1,0:T(8,128)S(1)}, u32[]{:S(2)}, u32[]{:S(2)}) collective-permute-start(f32[4,128,128]{2,1,0:T(8,128)} %multiply_add_fusion.5), channel_id=1, source_target_pairs={{8,0},{16,8},{24,16},{32,24},{40,32},{48,40},{56,48},{64,56},{72,6... | collective-permute-start | bytes 786440 | tf_op jit(solution)/shard_map/while/body/eval_jaxpr/ppermute | solution.py:13
  448.7 12.1 %collective-permute-start.1 = (f32[4,128,128]{2,1,0:T(8,128)}, f32[4,128,128]{2,1,0:T(8,128)S(1)}, u32[]{:S(2)}, u32[]{:S(2)}) collective-permute-start(f32[4,128,128]{2,1,0:T(8,128)} %multiply_add_fusion.5), channel_id=1, source_target_pairs={{8,0},{16,8},{24,16},{32,24},{40,32},{48,40},{56,48},{64,56},{72,6... | collective-permute-start | bytes 786440 | tf_op jit(solution)/shard_map/while/body/eval_jaxpr/ppermute | solution.py:13
  462.4 14.5 %collective-permute-start.1 = (f32[4,128,128]{2,1,0:T(8,128)}, f32[4,128,128]{2,1,0:T(8,128)S(1)}, u32[]{:S(2)}, u32[]{:S(2)}) collective-permute-start(f32[4,128,128]{2,1,0:T(8,128)} %multiply_add_fusion.5), channel_id=1, source_target_pairs={{8,0},{16,8},{24,16},{32,24},{40,32},{48,40},{56,48},{64,56},{72,6... | collective-permute-start | bytes 786440 | tf_op jit(solution)/shard_map/while/body/eval_jaxpr/ppermute | solution.py:13
  478.6 13.0 %collective-permute-start.1 = (f32[4,128,128]{2,1,0:T(8,128)}, f32[4,128,128]{2,1,0:T(8,128)S(1)}, u32[]{:S(2)}, u32[]{:S(2)}) collective-permute-start(f32[4,128,128]{2,1,0:T(8,128)} %multiply_add_fusion.5), channel_id=1, source_target_pairs={{8,0},{16,8},{24,16},{32,24},{40,32},{48,40},{56,48},{64,56},{72,6... | collective-permute-start | bytes 786440 | tf_op jit(solution)/shard_map/while/body/eval_jaxpr/ppermute | solution.py:13
  493.3 11.9 %collective-permute-start.1 = (f32[4,128,128]{2,1,0:T(8,128)}, f32[4,128,128]{2,1,0:T(8,128)S(1)}, u32[]{:S(2)}, u32[]{:S(2)}) collective-permute-start(f32[4,128,128]{2,1,0:T(8,128)} %multiply_add_fusion.5), channel_id=1, source_target_pairs={{8,0},{16,8},{24,16},{32,24},{40,32},{48,40},{56,48},{64,56},{72,6... | collective-permute-start | bytes 786440 | tf_op jit(solution)/shard_map/while/body/eval_jaxpr/ppermute | solution.py:13
  506.8 11.9 %collective-permute-start.1 = (f32[4,128,128]{2,1,0:T(8,128)}, f32[4,128,128]{2,1,0:T(8,128)S(1)}, u32[]{:S(2)}, u32[]{:S(2)}) collective-permute-start(f32[4,128,128]{2,1,0:T(8,128)} %multiply_add_fusion.5), channel_id=1, source_target_pairs={{8,0},{16,8},{24,16},{32,24},{40,32},{48,40},{56,48},{64,56},{72,6... | collective-permute-start | bytes 786440 | tf_op jit(solution)/shard_map/while/body/eval_jaxpr/ppermute | solution.py:13
  520.4 12.3 %collective-permute-start.1 = (f32[4,128,128]{2,1,0:T(8,128)}, f32[4,128,128]{2,1,0:T(8,128)S(1)}, u32[]{:S(2)}, u32[]{:S(2)}) collective-permute-start(f32[4,128,128]{2,1,0:T(8,128)} %multiply_add_fusion.5), channel_id=1, source_target_pairs={{8,0},{16,8},{24,16},{32,24},{40,32},{48,40},{56,48},{64,56},{72,6... | collective-permute-start | bytes 786440 | tf_op jit(solution)/shard_map/while/body/eval_jaxpr/ppermute | solution.py:13
  534.3 12.3 %collective-permute-start.1 = (f32[4,128,128]{2,1,0:T(8,128)}, f32[4,128,128]{2,1,0:T(8,128)S(1)}, u32[]{:S(2)}, u32[]{:S(2)}) collective-permute-start(f32[4,128,128]{2,1,0:T(8,128)} %multiply_add_fusion.5), channel_id=1, source_target_pairs={{8,0},{16,8},{24,16},{32,24},{40,32},{48,40},{56,48},{64,56},{72,6... | collective-permute-start | bytes 786440 | tf_op jit(solution)/shard_map/while/body/eval_jaxpr/ppermute | solution.py:13
  548.3 11.2 %collective-permute-start.1 = (f32[4,128,128]{2,1,0:T(8,128)}, f32[4,128,128]{2,1,0:T(8,128)S(1)}, u32[]{:S(2)}, u32[]{:S(2)}) collective-permute-start(f32[4,128,128]{2,1,0:T(8,128)} %multiply_add_fusion.5), channel_id=1, source_target_pairs={{8,0},{16,8},{24,16},{32,24},{40,32},{48,40},{56,48},{64,56},{72,6... | collective-permute-start | bytes 786440 | tf_op jit(solution)/shard_map/while/body/eval_jaxpr/ppermute | solution.py:13
  561.1 11.2 %collective-permute-start.1 = (f32[4,128,128]{2,1,0:T(8,128)}, f32[4,128,128]{2,1,0:T(8,128)S(1)}, u32[]{:S(2)}, u32[]{:S(2)}) collective-permute-start(f32[4,128,128]{2,1,0:T(8,128)} %multiply_add_fusion.5), channel_id=1, source_target_pairs={{8,0},{16,8},{24,16},{32,24},{40,32},{48,40},{56,48},{64,56},{72,6... | collective-permute-start | bytes 786440 | tf_op jit(solution)/shard_map/while/body/eval_jaxpr/ppermute | solution.py:13
  574.0 11.2 %collective-permute-start.1 = (f32[4,128,128]{2,1,0:T(8,128)}, f32[4,128,128]{2,1,0:T(8,128)S(1)}, u32[]{:S(2)}, u32[]{:S(2)}) collective-permute-start(f32[4,128,128]{2,1,0:T(8,128)} %multiply_add_fusion.5), channel_id=1, source_target_pairs={{8,0},{16,8},{24,16},{32,24},{40,32},{48,40},{56,48},{64,56},{72,6... | collective-permute-start | bytes 786440 | tf_op jit(solution)/shard_map/while/body/eval_jaxpr/ppermute | solution.py:13
  586.9 12.5 %collective-permute-start.1 = (f32[4,128,128]{2,1,0:T(8,128)}, f32[4,128,128]{2,1,0:T(8,128)S(1)}, u32[]{:S(2)}, u32[]{:S(2)}) collective-permute-start(f32[4,128,128]{2,1,0:T(8,128)} %multiply_add_fusion.5), channel_id=1, source_target_pairs={{8,0},{16,8},{24,16},{32,24},{40,32},{48,40},{56,48},{64,56},{72,6... | collective-permute-start | bytes 786440 | tf_op jit(solution)/shard_map/while/body/eval_jaxpr/ppermute | solution.py:13
  601.0 13.4 %collective-permute-start.1 = (f32[4,128,128]{2,1,0:T(8,128)}, f32[4,128,128]{2,1,0:T(8,128)S(1)}, u32[]{:S(2)}, u32[]{:S(2)}) collective-permute-start(f32[4,128,128]{2,1,0:T(8,128)} %multiply_add_fusion.5), channel_id=1, source_target_pairs={{8,0},{16,8},{24,16},{32,24},{40,32},{48,40},{56,48},{64,56},{72,6... | collective-permute-start | bytes 786440 | tf_op jit(solution)/shard_map/while/body/eval_jaxpr/ppermute | solution.py:13
  616.1 12.5 %collective-permute-start.1 = (f32[4,128,128]{2,1,0:T(8,128)}, f32[4,128,128]{2,1,0:T(8,128)S(1)}, u32[]{:S(2)}, u32[]{:S(2)}) collective-permute-start(f32[4,128,128]{2,1,0:T(8,128)} %multiply_add_fusion.5), channel_id=1, source_target_pairs={{8,0},{16,8},{24,16},{32,24},{40,32},{48,40},{56,48},{64,56},{72,6... | collective-permute-start | bytes 786440 | tf_op jit(solution)/shard_map/while/body/eval_jaxpr/ppermute | solution.py:13
  630.2 11.5 %collective-permute-start.1 = (f32[4,128,128]{2,1,0:T(8,128)}, f32[4,128,128]{2,1,0:T(8,128)S(1)}, u32[]{:S(2)}, u32[]{:S(2)}) collective-permute-start(f32[4,128,128]{2,1,0:T(8,128)} %multiply_add_fusion.5), channel_id=1, source_target_pairs={{8,0},{16,8},{24,16},{32,24},{40,32},{48,40},{56,48},{64,56},{72,6... | collective-permute-start | bytes 786440 | tf_op jit(solution)/shard_map/while/body/eval_jaxpr/ppermute | solution.py:13
  643.4 10.7 %collective-permute-start.1 = (f32[4,128,128]{2,1,0:T(8,128)}, f32[4,128,128]{2,1,0:T(8,128)S(1)}, u32[]{:S(2)}, u32[]{:S(2)}) collective-permute-start(f32[4,128,128]{2,1,0:T(8,128)} %multiply_add_fusion.5), channel_id=1, source_target_pairs={{8,0},{16,8},{24,16},{32,24},{40,32},{48,40},{56,48},{64,56},{72,6... | collective-permute-start | bytes 786440 | tf_op jit(solution)/shard_map/while/body/eval_jaxpr/ppermute | solution.py:13
  655.7 10.6 %collective-permute-start.1 = (f32[4,128,128]{2,1,0:T(8,128)}, f32[4,128,128]{2,1,0:T(8,128)S(1)}, u32[]{:S(2)}, u32[]{:S(2)}) collective-permute-start(f32[4,128,128]{2,1,0:T(8,128)} %multiply_add_fusion.5), channel_id=1, source_target_pairs={{8,0},{16,8},{24,16},{32,24},{40,32},{48,40},{56,48},{64,56},{72,6... | collective-permute-start | bytes 786440 | tf_op jit(solution)/shard_map/while/body/eval_jaxpr/ppermute | solution.py:13
  668.0 11.5 %collective-permute-start.1 = (f32[4,128,128]{2,1,0:T(8,128)}, f32[4,128,128]{2,1,0:T(8,128)S(1)}, u32[]{:S(2)}, u32[]{:S(2)}) collective-permute-start(f32[4,128,128]{2,1,0:T(8,128)} %multiply_add_fusion.5), channel_id=1, source_target_pairs={{8,0},{16,8},{24,16},{32,24},{40,32},{48,40},{56,48},{64,56},{72,6... | collective-permute-start | bytes 786440 | tf_op jit(solution)/shard_map/while/body/eval_jaxpr/ppermute | solution.py:13
  681.2 13.2 %collective-permute-start.1 = (f32[4,128,128]{2,1,0:T(8,128)}, f32[4,128,128]{2,1,0:T(8,128)S(1)}, u32[]{:S(2)}, u32[]{:S(2)}) collective-permute-start(f32[4,128,128]{2,1,0:T(8,128)} %multiply_add_fusion.5), channel_id=1, source_target_pairs={{8,0},{16,8},{24,16},{32,24},{40,32},{48,40},{56,48},{64,56},{72,6... | collective-permute-start | bytes 786440 | tf_op jit(solution)/shard_map/while/body/eval_jaxpr/ppermute | solution.py:13
  696.1 10.6 %collective-permute-start.1 = (f32[4,128,128]{2,1,0:T(8,128)}, f32[4,128,128]{2,1,0:T(8,128)S(1)}, u32[]{:S(2)}, u32[]{:S(2)}) collective-permute-start(f32[4,128,128]{2,1,0:T(8,128)} %multiply_add_fusion.5), channel_id=1, source_target_pairs={{8,0},{16,8},{24,16},{32,24},{40,32},{48,40},{56,48},{64,56},{72,6... | collective-permute-start | bytes 786440 | tf_op jit(solution)/shard_map/while/body/eval_jaxpr/ppermute | solution.py:13
  708.3 10.9 %collective-permute-start.1 = (f32[4,128,128]{2,1,0:T(8,128)}, f32[4,128,128]{2,1,0:T(8,128)S(1)}, u32[]{:S(2)}, u32[]{:S(2)}) collective-permute-start(f32[4,128,128]{2,1,0:T(8,128)} %multiply_add_fusion.5), channel_id=1, source_target_pairs={{8,0},{16,8},{24,16},{32,24},{40,32},{48,40},{56,48},{64,56},{72,6... | collective-permute-start | bytes 786440 | tf_op jit(solution)/shard_map/while/body/eval_jaxpr/ppermute | solution.py:13
  720.9 12.0 %collective-permute-start.1 = (f32[4,128,128]{2,1,0:T(8,128)}, f32[4,128,128]{2,1,0:T(8,128)S(1)}, u32[]{:S(2)}, u32[]{:S(2)}) collective-permute-start(f32[4,128,128]{2,1,0:T(8,128)} %multiply_add_fusion.5), channel_id=1, source_target_pairs={{8,0},{16,8},{24,16},{32,24},{40,32},{48,40},{56,48},{64,56},{72,6... | collective-permute-start | bytes 786440 | tf_op jit(solution)/shard_map/while/body/eval_jaxpr/ppermute | solution.py:13
  734.5 13.1 %collective-permute-start.1 = (f32[4,128,128]{2,1,0:T(8,128)}, f32[4,128,128]{2,1,0:T(8,128)S(1)}, u32[]{:S(2)}, u32[]{:S(2)}) collective-permute-start(f32[4,128,128]{2,1,0:T(8,128)} %multiply_add_fusion.5), channel_id=1, source_target_pairs={{8,0},{16,8},{24,16},{32,24},{40,32},{48,40},{56,48},{64,56},{72,6... | collective-permute-start | bytes 786440 | tf_op jit(solution)/shard_map/while/body/eval_jaxpr/ppermute | solution.py:13
  749.3 12.5 %collective-permute-start.1 = (f32[4,128,128]{2,1,0:T(8,128)}, f32[4,128,128]{2,1,0:T(8,128)S(1)}, u32[]{:S(2)}, u32[]{:S(2)}) collective-permute-start(f32[4,128,128]{2,1,0:T(8,128)} %multiply_add_fusion.5), channel_id=1, source_target_pairs={{8,0},{16,8},{24,16},{32,24},{40,32},{48,40},{56,48},{64,56},{72,6... | collective-permute-start | bytes 786440 | tf_op jit(solution)/shard_map/while/body/eval_jaxpr/ppermute | solution.py:13
  763.5 11.7 %collective-permute-start.1 = (f32[4,128,128]{2,1,0:T(8,128)}, f32[4,128,128]{2,1,0:T(8,128)S(1)}, u32[]{:S(2)}, u32[]{:S(2)}) collective-permute-start(f32[4,128,128]{2,1,0:T(8,128)} %multiply_add_fusion.5), channel_id=1, source_target_pairs={{8,0},{16,8},{24,16},{32,24},{40,32},{48,40},{56,48},{64,56},{72,6... | collective-permute-start | bytes 786440 | tf_op jit(solution)/shard_map/while/body/eval_jaxpr/ppermute | solution.py:13
  776.9 10.6 %collective-permute-start.1 = (f32[4,128,128]{2,1,0:T(8,128)}, f32[4,128,128]{2,1,0:T(8,128)S(1)}, u32[]{:S(2)}, u32[]{:S(2)}) collective-permute-start(f32[4,128,128]{2,1,0:T(8,128)} %multiply_add_fusion.5), channel_id=1, source_target_pairs={{8,0},{16,8},{24,16},{32,24},{40,32},{48,40},{56,48},{64,56},{72,6... | collective-permute-start | bytes 786440 | tf_op jit(solution)/shard_map/while/body/eval_jaxpr/ppermute | solution.py:13
  789.1 10.6 %collective-permute-start.1 = (f32[4,128,128]{2,1,0:T(8,128)}, f32[4,128,128]{2,1,0:T(8,128)S(1)}, u32[]{:S(2)}, u32[]{:S(2)}) collective-permute-start(f32[4,128,128]{2,1,0:T(8,128)} %multiply_add_fusion.5), channel_id=1, source_target_pairs={{8,0},{16,8},{24,16},{32,24},{40,32},{48,40},{56,48},{64,56},{72,6... | collective-permute-start | bytes 786440 | tf_op jit(solution)/shard_map/while/body/eval_jaxpr/ppermute | solution.py:13
  801.4 10.6 %collective-permute-start.1 = (f32[4,128,128]{2,1,0:T(8,128)}, f32[4,128,128]{2,1,0:T(8,128)S(1)}, u32[]{:S(2)}, u32[]{:S(2)}) collective-permute-start(f32[4,128,128]{2,1,0:T(8,128)} %multiply_add_fusion.5), channel_id=1, source_target_pairs={{8,0},{16,8},{24,16},{32,24},{40,32},{48,40},{56,48},{64,56},{72,6... | collective-permute-start | bytes 786440 | tf_op jit(solution)/shard_map/while/body/eval_jaxpr/ppermute | solution.py:13
  813.6 10.6 %collective-permute-start.1 = (f32[4,128,128]{2,1,0:T(8,128)}, f32[4,128,128]{2,1,0:T(8,128)S(1)}, u32[]{:S(2)}, u32[]{:S(2)}) collective-permute-start(f32[4,128,128]{2,1,0:T(8,128)} %multiply_add_fusion.5), channel_id=1, source_target_pairs={{8,0},{16,8},{24,16},{32,24},{40,32},{48,40},{56,48},{64,56},{72,6... | collective-permute-start | bytes 786440 | tf_op jit(solution)/shard_map/while/body/eval_jaxpr/ppermute | solution.py:13
  825.9 10.6 %collective-permute-start.1 = (f32[4,128,128]{2,1,0:T(8,128)}, f32[4,128,128]{2,1,0:T(8,128)S(1)}, u32[]{:S(2)}, u32[]{:S(2)}) collective-permute-start(f32[4,128,128]{2,1,0:T(8,128)} %multiply_add_fusion.5), channel_id=1, source_target_pairs={{8,0},{16,8},{24,16},{32,24},{40,32},{48,40},{56,48},{64,56},{72,6... | collective-permute-start | bytes 786440 | tf_op jit(solution)/shard_map/while/body/eval_jaxpr/ppermute | solution.py:13
  875.3 125.4 %collective-permute-start.3 = (f32[3,3,512]{2,1,0:T(4,128)S(1)}, f32[3,3,512]{2,1,0:T(4,128)S(1)}, u32[]{:S(2)}, u32[]{:S(2)}) collective-permute-start(f32[3,3,512]{2,1,0:T(4,128)S(1)} %slice.112), channel_id=1, source_target_pairs={{8,0},{16,8},{24,16},{32,24},{40,32},{48,40},{56,48},{64,56},{72,6... | collective-permute-start | bytes 55304 | tf_op jit(solution)/shard_map/ppermute | solution.py:13
  (16 other events, 571.1 us)
Sparse Core Ops, SparseCore 0:
  9.8 37.5 all-gather.1
  412.3 36.3 reduce-scatter.2
  453.3 251.1 reduce-scatter.4
where the time goes:
time: 1030 us; the launch traced here: 1010 us
  waiting for transfers between devices  454 us (44%)
  starting transfers between devices  266 us (26%)
  blocking collectives  118 us (11%)
  other arithmetic  73.5 us (7%)
  matrix products  68.2 us (7%)
  between operations  15.7 us (2%)
  local copies, waits for them, and re-layouts  13.9 us (1%)
    ppermute x64, waiting for transfers between devices, from_behind(): return lax.ppermute(array, axis, pairs)  454 us
    ppermute x64, starting transfers between devices, from_behind(): return lax.ppermute(array, axis, pairs)  266 us
    psum x1, blocking collectives, body(): grad_conv = lax.psum(jnp.stack(tap_sums, axis=1), 'seq')  118 us
    add x62, other arithmetic, advance(): return moving(local + (1.0 - resets) * incoming)  53 us
  transfers between devices with their start and end apart: 67, of which 62 were waited for; matrix products, arithmetic and copies ran while one was open for 13% of the time, Pallas kernels for 0%

commit v1 on v0

--- a/solution.py
+++ b/solution.py
@@ -18,24 +18,13 @@
     return counted - 1
 
 
-def pass_along(resets, local, length, moving):
-
-    def advance(number, incoming):
-        return moving(local + (1.0 - resets) * incoming)
-
-    return lax.fori_loop(0, length, advance, jnp.zeros_like(local))
-
-
-def carry_forward(resets, local):
-    return pass_along(
-        resets, local, lax.axis_size("seq") - 1, lambda moving: from_behind(moving, "seq", 1)
-    )
-
-
-def carry_backward(resets, local):
-    return pass_along(
-        resets, local, lax.axis_size("seq") - 1, lambda moving: from_behind(moving, "seq", -1)
-    )
+def window_carry(local, doc_end, step):
+    total = from_behind(local, "seq", step)
+    reach = 1
+    while reach < 8:
+        total = total + doc_end(reach) * from_behind(total, "seq", step * reach)
+        reach *= 2
+    return total
 
 
 def feature_map(field):
@@ -50,11 +39,15 @@
     tok_rows = projected.shape[1]
     channels = projected.shape[2]
     head_count = channels // DH
-    high = lax.Precision.HIGHEST
+    high = lax.Precision.DEFAULT
     offset = lax.axis_index("seq") * tok_rows
     doc_starts = jnp.cumsum(doc_lengths) - doc_lengths
     positions = offset + jnp.arange(-(KW - 1), tok_rows + KW - 1, dtype=jnp.int32)
     doc_all = segment_of(doc_starts, positions)
+    block_ends = offset + tok_rows * jnp.arange(-8, 9, dtype=jnp.int32) - 1
+    doc_at = segment_of(doc_starts, block_ends)
+    behind = lambda reach: (doc_at[8] == doc_at[8 - reach]).astype(jnp.float32)
+    ahead_of = lambda reach: (doc_at[9] == doc_at[9 + reach]).astype(jnp.float32)
     doc_here = doc_all[KW - 1 : KW - 1 + tok_rows]
     doc_before = doc_all[KW - 2]
     doc_last = doc_all[KW - 2 + tok_rows]
@@ -85,9 +78,8 @@
     head_mask = (doc_here == doc_before).astype(jnp.float32)[:, None, None]
     tail_keep = doc_here == doc_last
     tail_mask = tail_keep.astype(jnp.float32)[:, None, None]
-    resets = (doc_last != doc_before).astype(jnp.float32)
     tail_state = jnp.einsum("thd,the->hde", key_float * tail_mask, value_float, precision=high)
-    state_in = carry_forward(resets, tail_state)
+    state_in = window_carry(tail_state, behind, 1)
     outputs = local_out + head_mask * jnp.einsum(
         "thd,hde->the", query_float, state_in, precision=high
     )
@@ -109,11 +101,11 @@
     grad_out_weight = lax.psum_scatter(
         lax.dot_general(
             columns, normed, (((0,), (0,)), ((), ())), preferred_element_type=jnp.float32
-        ),
+        ).astype(jnp.bfloat16),
         "seq",
         scatter_dimension=0,
         tiled=True,
-    ).T
+    ).astype(jnp.float32).T
     grad_unit = lax.dot_general(
         full_grad, out_weight, (((1,), (1,)), ((), ())), preferred_element_type=jnp.float32
     )
@@ -123,7 +115,7 @@
         allowed[None], jnp.einsum("thd,shd->hts", grad_outputs, value_float, precision=high), 0.0
     )
     grad_back = jnp.einsum("thd,the->hde", query_float * head_mask, grad_outputs, precision=high)
-    state_out = carry_backward(resets, grad_back)
+    state_out = window_carry(grad_back, ahead_of, -1)
     grad_query = jnp.einsum("hts,shd->thd", grad_weights, key_float, precision=high)
     grad_query = grad_query + head_mask * jnp.einsum(
         "the,hde->thd", grad_outputs, state_in, precision=high

time: 1030 us -> 381 us (0.37); the launches traced: 1010 us -> 379 us
  waiting for transfers between devices: 454 us -> 110 us
  starting transfers between devices: 266 us -> 49.3 us
  other arithmetic: 73.5 us -> 23.7 us
  matrix products: 68.2 us -> 34.4 us
    ppermute x64 -> x10, waiting for transfers between devices: 454 us -> 60.7 us  [from_behind(): return lax.ppermute(array, axis, pairs)]
    ppermute x64 -> x10, starting transfers between devices: 266 us -> 49 us  [from_behind(): return lax.ppermute(array, axis, pairs)]
    add x62 -> x4, other arithmetic: 53 us -> 2.1 us  [window_carry(): total = total + doc_end(reach) * from_behind(total, 'seq', step * reach)]
    reduce_scatter x1, waiting for transfers between devices: 0.01 us -> 41.1 us  [body(): lax.psum_scatter(lax.dot_general(columns, normed, (((0,), (1,)), ((), ())...]
  transfers between devices with their start and end apart: 67 -> 13, of which waited for: 62 -> 11; matrix products, arithmetic and copies ran while one was open for 13% -> 15% of each run, Pallas kernels for 0% -> 0%
where the time goes in v1:
time: 381 us; the launch traced here: 379 us
  blocking collectives  122 us (32%)
  waiting for transfers between devices  110 us (29%)
  starting transfers between devices  49.3 us (13%)
  matrix products  34.4 us (9%)
  other arithmetic  23.7 us (6%)
  between operations  21.7 us (6%)
  local copies, waits for them, and re-layouts  18.7 us (5%)
    psum x1, blocking collectives, body(): grad_conv = lax.psum(jnp.stack(tap_sums, axis=1), 'seq')  122 us
    ppermute x10, waiting for transfers between devices, from_behind(): return lax.ppermute(array, axis, pairs)  60.7 us
    ppermute x10, starting transfers between devices, from_behind(): return lax.ppermute(array, axis, pairs)  49 us
    reduce_scatter x1, waiting for transfers between devices, body(): lax.psum_scatter(lax.dot_general(columns, normed, (((0,), (1,)), ((), ())...  41.1 us
    unnamed x35, local copies, waits for them, and re-layouts  8.86 us
    unnamed x4, waiting for transfers between devices  8.08 us
  transfers between devices with their start and end apart: 13, of which 11 were waited for; matrix products, arithmetic and copies ran while one was open for 15% of the time, Pallas kernels for 0%

profile of v1, /device:TPU:6, one launch (start us, length us, event | category | flops | bytes accessed | tf_op | source)
XLA Modules:
  0.0 379.4 jit_solution(13373892587046622400)
XLA Ops:
  7.2 0.7 all-gather.2.cloned.1.call-update
  7.9 0.8 slice.111
  8.7 3.8 %collective-permute-start = (bf16[3,3,512]{2,1,0:T(4,128)(2,1)S(1)}, bf16[3,3,512]{2,1,0:T(4,128)(2,1)S(1)}, u32[]{:S(2)}, u32[]{:S(2)}) collective-permute-start(bf16[3,3,512]{2,1,0:T(4,128)(2,1)S(1)} %slice.111), channel_id=1, source_target_pairs={{0,8},{8,16},{16,24},{24,32},{32,40},{40,48},{48,56},{56,64},{64,7... | collective-permute-start | bytes 27656 | tf_op jit(solution)/shard_map/ppermute | solution.py:13
  12.5 0.8 reduce-window.9
  13.4 0.7 bitcast_subtract_fusion
  14.1 0.6 fusion.87
  14.7 0.9 fusion.86
  15.7 1.4 fusion.67
  17.0 1.4 collective-permute-done
  18.4 5.0 %fusion.13 = bf16[3,512,512]{2,1,0:T(8,128)(2,1)S(1)} fusion(bf16[3,512,512]{2,1,0:T(8,128)(2,1)} %param.5, bf16[3,3,512]{2,1,0:T(4,128)(2,1)S(1)} %collective-permute-done, f32[512]{0:T(512)S(1)} %get-tuple-element.35, f32[3,512]{1,0:T(4,128)S(1)} %get-tuple-element.51, f32[512]{0:T(512)S(1)} %get-tuple-element.36, f32[3,512]{1,0:T(4,128)S(1)} %get-tuple-element.52, ...), kind=kLoop, calls=%fused_computation.24 | loop fusion | flops 18874368 | bytes 3185664 | tf_op jit(solution)/shard_map/convert_element_type | solution.py:67
  23.4 1.3 slice_convert_fusion.1
  24.7 0.3 copy.67
  25.3 0.6 fusion.58
  25.9 2.5 collective-permute-start.1
  28.5 8.6 %collective-permute-done.1 = f32[4,128,128]{2,1,0:T(8,128)S(1)} collective-permute-done((f32[4,128,128]{2,1,0:T(8,128)S(1)}, f32[4,128,128]{2,1,0:T(8,128)S(1)}, u32[]{:S(2)}, u32[]{:S(2)}) %collective-permute-start.1) | collective-permute-done | bytes 262176 | tf_op jit(solution)/shard_map/ppermute | solution.py:13
  37.1 1.9 collective-permute-start.2
  39.0 0.6 fusion.88
  40.8 6.6 %collective-permute-done.2 = f32[4,128,128]{2,1,0:T(8,128)S(1)} collective-permute-done((f32[4,128,128]{2,1,0:T(8,128)S(1)}, f32[4,128,128]{2,1,0:T(8,128)S(1)}, u32[]{:S(2)}, u32[]{:S(2)}) %collective-permute-start.2) | collective-permute-done | bytes 262176 | tf_op jit(solution)/shard_map/ppermute | solution.py:13
  47.5 1.9 collective-permute-start.3
  52.2 1.7 copy.66
  53.9 8.3 %collective-permute-done.3 = f32[4,128,128]{2,1,0:T(8,128)S(1)} collective-permute-done((f32[4,128,128]{2,1,0:T(8,128)S(1)}, f32[4,128,128]{2,1,0:T(8,128)S(1)}, u32[]{:S(2)}, u32[]{:S(2)}) %collective-permute-start.3) | collective-permute-done | bytes 262176 | tf_op jit(solution)/shard_map/ppermute | solution.py:13
  62.2 0.7 copy-done.14
  62.9 1.0 multiply_add_fusion.4
  63.9 6.9 %collective-permute-start.4 = (f32[4,128,128]{2,1,0:T(8,128)S(1)}, f32[4,128,128]{2,1,0:T(8,128)S(1)}, u32[]{:S(2)}, u32[]{:S(2)}) collective-permute-start(f32[4,128,128]{2,1,0:T(8,128)S(1)} %multiply_add_fusion.4), channel_id=1, source_target_pairs={{0,32},{8,40},{16,48},{24,56},{32,64},{40,72},{48,80},{56,88},{64,... | collective-permute-start | bytes 786440 | tf_op jit(solution)/shard_map/ppermute | solution.py:13
  70.8 1.3 fusion.80
  72.2 10.7 %collective-permute-done.4 = f32[4,128,128]{2,1,0:T(8,128)S(1)} collective-permute-done((f32[4,128,128]{2,1,0:T(8,128)S(1)}, f32[4,128,128]{2,1,0:T(8,128)S(1)}, u32[]{:S(2)}, u32[]{:S(2)}) %collective-permute-start.4) | collective-permute-done | bytes 262176 | tf_op jit(solution)/shard_map/ppermute | solution.py:13
  82.9 0.7 convolution_multiply_fusion.3
  83.6 1.8 fusion.55
  85.4 7.2 %multiply_reduce_fusion = (f32[512,4]{0,1:T(4,128)S(1)}, bf16[512,4,128]{0,2,1:T(8,128)(2,1)S(1)}, f32[512,512]{0,1:T(8,128)}) fusion(f32[4,128,512]{2,1,0:T(8,128)} %get-tuple-element.49, f32[512,4]{0,1:T(4,128)S(1)} %add_rsqrt_fusion, bf16[512,4096]{1,0:T(8,128)(2,1)} %all-gather.2.cloned.1.call-done, bf16[512,4096]{1,0:T(8,128)(2,1)} %param.7), kind=kOutput, calls=%fused_computation.87 | convolution fusion | flops 2148530176 | bytes 11026432 | tf_op jit(solution)/shard_map/dot_general | solution.py:109
  92.6 4.3 %fusion.1 = bf16[4096,512]{0,1:T(8,128)(2,1)} fusion(bf16[512,512]{0,1:T(8,128)(2,1)S(1)} %bitcast.97, bf16[512,4096]{1,0:T(8,128)(2,1)S(1)} %copy-done.4), kind=kOutput, calls=%fused_computation.3 | convolution fusion | flops 2149580800 | bytes 8912896 | tf_op jit(solution)/shard_map/dot_general | solution.py:102
  96.9 6.5 %copy.96 = bf16[4096,512]{1,0:T(8,128)(2,1)} copy(bf16[4096,512]{0,1:T(8,128)(2,1)} %fusion.1) | data formatting | bytes 8388608
  103.4 0.2 reduce-scatter.5.cloned.1.call-start
  103.7 6.5 %fusion = bf16[4096,512]{0,1:T(8,128)(2,1)} fusion(bf16[512,512]{0,1:T(8,128)(2,1)S(1)} %bitcast.98, bf16[512,4096]{1,0:T(8,128)(2,1)} %param.7), kind=kOutput, calls=%fused_computation.2 | convolution fusion | flops 2149580800 | bytes 8912896 | tf_op jit(solution)/shard_map/dot_general | solution.py:91
  114.0 1.8 subtract_multiply_fusion
  115.8 0.6 fusion.56
  116.4 1.9 collective-permute-start.5
  118.4 0.7 fusion.89
  119.2 0.9 fusion.4
  120.0 6.7 %collective-permute-done.5 = f32[4,128,128]{2,1,0:T(8,128)} collective-permute-done((f32[4,128,128]{2,1,0:T(8,128)S(1)}, f32[4,128,128]{2,1,0:T(8,128)}, u32[]{:S(2)}, u32[]{:S(2)}) %collective-permute-start.5) | collective-permute-done | bytes 262176 | tf_op jit(solution)/shard_map/ppermute | solution.py:13
  126.8 4.8 %collective-permute-start.6 = (f32[4,128,128]{2,1,0:T(8,128)}, f32[4,128,128]{2,1,0:T(8,128)}, u32[]{:S(2)}, u32[]{:S(2)}) collective-permute-start(f32[4,128,128]{2,1,0:T(8,128)} %collective-permute-done.5), channel_id=1, source_target_pairs={{8,0},{16,8},{24,16},{32,24},{40,32},{48,40},{56,48},{64,56},{72,6... | collective-permute-start | bytes 786440 | tf_op jit(solution)/shard_map/ppermute | solution.py:13
  131.6 1.4 fusion.50
  133.0 1.6 copy.80
  134.5 3.3 collective-permute-done.6
  137.9 1.1 multiply_add_fusion.2
  139.0 4.3 %collective-permute-start.7 = (f32[4,128,128]{2,1,0:T(8,128)S(1)}, f32[4,128,128]{2,1,0:T(8,128)S(1)}, u32[]{:S(2)}, u32[]{:S(2)}) collective-permute-start(f32[4,128,128]{2,1,0:T(8,128)S(1)} %multiply_add_fusion.2), channel_id=1, source_target_pairs={{16,0},{24,8},{32,16},{40,24},{48,32},{56,40},{64,48},{72,56},{80,... | collective-permute-start | bytes 786440 | tf_op jit(solution)/shard_map/ppermute | solution.py:13
  143.3 2.3 fusion.44
  145.6 6.2 %collective-permute-done.7 = f32[4,128,128]{2,1,0:T(8,128)S(1)} collective-permute-done((f32[4,128,128]{2,1,0:T(8,128)S(1)}, f32[4,128,128]{2,1,0:T(8,128)S(1)}, u32[]{:S(2)}, u32[]{:S(2)}) %collective-permute-start.7) | collective-permute-done | bytes 262176 | tf_op jit(solution)/shard_map/ppermute | solution.py:13
  151.8 4.3 %collective-permute-start.8 = (f32[4,128,128]{2,1,0:T(8,128)S(1)}, f32[4,128,128]{2,1,0:T(8,128)S(1)}, u32[]{:S(2)}, u32[]{:S(2)}) collective-permute-start(f32[4,128,128]{2,1,0:T(8,128)S(1)} %multiply_add_fusion.1), channel_id=1, source_target_pairs={{32,0},{40,8},{48,16},{56,24},{64,32},{72,40},{80,48},{88,56},{96,... | collective-permute-start | bytes 786440 | tf_op jit(solution)/shard_map/ppermute | solution.py:13
  156.2 1.5 fusion.6
  157.7 8.8 %collective-permute-done.8 = f32[4,128,128]{2,1,0:T(8,128)S(1)} collective-permute-done((f32[4,128,128]{2,1,0:T(8,128)S(1)}, f32[4,128,128]{2,1,0:T(8,128)S(1)}, u32[]{:S(2)}, u32[]{:S(2)}) %collective-permute-start.8) | collective-permute-done | bytes 262176 | tf_op jit(solution)/shard_map/ppermute | solution.py:13
  166.5 1.5 fusion.43
  168.0 1.6 copy.81
  169.6 3.0 fusion.47
  172.6 1.6 copy.82
  174.1 6.1 %fusion.17 = (f32[3,512]{1,0:T(4,128)S(1)}, f32[3,512]{1,0:T(4,128)S(1)}, f32[3,512]{1,0:T(4,128)S(1)}, f32[3,512]{1,0:T(4,128)S(1)}, f32[3,512,512]{2,1,0:T(8,128)S(1)}) fusion(f32[512]{0:T(512)S(1)} %get-tuple-element.37, bf16[3,512,512]{2,1,0:T(8,128)(2,1)} %param.5, bf16[3,3,512]{2,1,0:T(4,128)(2,1)S(1)} %collective-permute-done, ...), kind=kLoop, calls=%fused_computation.28 | loop fusion | flops 20441088 | bytes 7904256 | tf_op jit(solution)/shard_map/reduce_sum | solution.py:149
  180.2 16.7 %collective-permute-start.9 = (f32[3,3,512]{2,1,0:T(4,128)S(1)}, f32[3,3,512]{2,1,0:T(4,128)S(1)}, u32[]{:S(2)}, u32[]{:S(2)}) collective-permute-start(f32[3,3,512]{2,1,0:T(4,128)S(1)} %slice.148), channel_id=1, source_target_pairs={{8,0},{16,8},{24,16},{32,24},{40,32},{48,40},{56,48},{64,56},{72,6... | collective-permute-start | bytes 55304 | tf_op jit(solution)/shard_map/ppermute | solution.py:13
  196.9 121.7 %psum.7 = f32[3,4,512]{2,0,1:T(4,128)S(1)} all-reduce(f32[3,4,512]{2,0,1:T(4,128)S(1)} %pad_maximum_fusion.3), channel_id=1, replica_groups=mesh['seq'=32,'head'=8] {'seq'}, use_global_device_ids=true, to_apply=%region_10.11 | all-reduce | flops 6144 | bytes 49152 | tf_op jit(solution)/shard_map/psum | solution.py:150
  318.7 0.6 copy.83
  319.3 0.4 pad_maximum_fusion
  319.7 3.0 fusion.26
  322.7 7.4 %reduce-scatter.7.cloned.1.call-done = bf16[128,512]{1,0:T(8,128)(2,1)} async-done(((bf16[4096,512]{1,0:T(8,128)(2,1)}), bf16[128,512]{1,0:T(8,128)(2,1)}) %reduce-scatter.7.cloned.1.call-update) | async-done | bytes 131088
  330.1 1.0 copy.97
  331.1 0.7 convert_bitcast_fusion
  331.9 41.1 %reduce-scatter.5.cloned.1.call-done = bf16[512,512]{0,1:T(8,128)(2,1)} async-done(((bf16[4096,512]{0,1:T(8,128)(2,1)}), bf16[512,512]{0,1:T(8,128)(2,1)}) %reduce-scatter.5.cloned.1.call-update) | async-done | bytes 524304 | tf_op jit(solution)/shard_map/reduce_scatter | solution.py:90
  (52 shorter events, 1.0 us)
Async XLA Ops:
  7.2 78.3 %all-gather.2.cloned.1.call-start = ((), (), s32[]{:S(2)}) async-start(), calls=%async_computation.3 | async-start | bytes 4718592 | tf_op jit(solution)/shard_map/all_gather | solution.py:99
  7.9 322.2 %reduce-scatter.7.cloned.1.call-start = ((), (), s32[]{:S(2)}) async-start(), calls=%async_computation.4 | async-start | bytes 4325376
  8.7 9.7 %collective-permute-start = (bf16[3,3,512]{2,1,0:T(4,128)(2,1)S(1)}, bf16[3,3,512]{2,1,0:T(4,128)(2,1)S(1)}, u32[]{:S(2)}, u32[]{:S(2)}) collective-permute-start(bf16[3,3,512]{2,1,0:T(4,128)(2,1)S(1)} %slice.111), channel_id=1, source_target_pairs={{0,8},{8,16},{16,24},{24,32},{32,40},{40,48},{48,56},{56,64},{64,7... | collective-permute-start | bytes 27656 | tf_op jit(solution)/shard_map/ppermute | solution.py:13
  25.3 93.1 %copy-start.2 = (bf16[1,512,512]{1,2,0:T(8,128)(2,1)}, bf16[1,512,512]{1,2,0:T(8,128)(2,1)S(1)}, u32[]{:S(2)}) copy-start(bf16[1,512,512]{1,2,0:T(8,128)(2,1)S(1)} %copy.65) | copy-start | bytes 1572868
  25.9 11.2 %collective-permute-start.1 = (f32[4,128,128]{2,1,0:T(8,128)S(1)}, f32[4,128,128]{2,1,0:T(8,128)S(1)}, u32[]{:S(2)}, u32[]{:S(2)}) collective-permute-start(f32[4,128,128]{2,1,0:T(8,128)S(1)} %fusion.58), channel_id=1, source_target_pairs={{0,8},{8,16},{16,24},{24,32},{32,40},{40,48},{48,56},{56,64},{64,7... | collective-permute-start | bytes 786440 | tf_op jit(solution)/shard_map/ppermute | solution.py:13
  37.1 10.4 %collective-permute-start.2 = (f32[4,128,128]{2,1,0:T(8,128)S(1)}, f32[4,128,128]{2,1,0:T(8,128)S(1)}, u32[]{:S(2)}, u32[]{:S(2)}) collective-permute-start(f32[4,128,128]{2,1,0:T(8,128)S(1)} %collective-permute-done.1), channel_id=1, source_target_pairs={{0,8},{8,16},{16,24},{24,32},{32,40},{40,48},{48,56},{56,64},{64,7... | collective-permute-start | bytes 786440 | tf_op jit(solution)/shard_map/ppermute | solution.py:13
  47.5 14.8 %collective-permute-start.3 = (f32[4,128,128]{2,1,0:T(8,128)S(1)}, f32[4,128,128]{2,1,0:T(8,128)S(1)}, u32[]{:S(2)}, u32[]{:S(2)}) collective-permute-start(f32[4,128,128]{2,1,0:T(8,128)S(1)} %multiply_add_fusion.5), channel_id=1, source_target_pairs={{0,16},{8,24},{16,32},{24,40},{32,48},{40,56},{48,64},{56,72},{64,... | collective-permute-start | bytes 786440 | tf_op jit(solution)/shard_map/ppermute | solution.py:13
  52.2 31.4 %copy-start.11 = (pred[512,512]{1,0:T(8,128)(4,1)}, pred[512,512]{1,0:T(8,128)(4,1)S(1)}, u32[]{:S(2)}) copy-start(pred[512,512]{1,0:T(8,128)(4,1)S(1)} %fusion.60) | copy-start | bytes 786436
  62.2 0.7 copy-start.14
  63.9 19.0 %collective-permute-start.4 = (f32[4,128,128]{2,1,0:T(8,128)S(1)}, f32[4,128,128]{2,1,0:T(8,128)S(1)}, u32[]{:S(2)}, u32[]{:S(2)}) collective-permute-start(f32[4,128,128]{2,1,0:T(8,128)S(1)} %multiply_add_fusion.4), channel_id=1, source_target_pairs={{0,32},{8,40},{16,48},{24,56},{32,64},{40,72},{48,80},{56,88},{64,... | collective-permute-start | bytes 786440 | tf_op jit(solution)/shard_map/ppermute | solution.py:13
  72.2 13.2 %copy-start.6 = (bf16[4,512,512]{2,1,0:T(8,128)(2,1)}, bf16[4,512,512]{2,1,0:T(8,128)(2,1)S(1)}, u32[]{:S(2)}) copy-start(bf16[4,512,512]{2,1,0:T(8,128)(2,1)S(1)} %fusion.80) | copy-start | bytes 6291460
  82.9 2.5 copy-start.8
  85.4 7.2 %copy-start.4 = (bf16[512,4096]{1,0:T(8,128)(2,1)S(1)}, bf16[512,4096]{1,0:T(8,128)(2,1)}, u32[]{:S(2)}) copy-start(bf16[512,4096]{1,0:T(8,128)(2,1)} %all-gather.2.cloned.1.call-done) | copy-start | bytes 12582916
  103.4 269.5 %reduce-scatter.5.cloned.1.call-start = ((), (), s32[]{:S(2)}) async-start(), calls=%async_computation.2 | async-start | bytes 4718592 | tf_op jit(solution)/shard_map/reduce_scatter | solution.py:90
  115.8 15.7 %copy-start = (bf16[512,4,128]{0,2,1:T(8,128)(2,1)}, bf16[512,4,128]{0,2,1:T(8,128)(2,1)S(1)}, u32[]{:S(2)}) copy-start(bf16[512,4,128]{0,2,1:T(8,128)(2,1)S(1)} %subtract_multiply_fusion) | copy-start | bytes 1572868
  115.8 3.3 copy-start.12
  116.4 10.4 %collective-permute-start.5 = (f32[4,128,128]{2,1,0:T(8,128)S(1)}, f32[4,128,128]{2,1,0:T(8,128)}, u32[]{:S(2)}, u32[]{:S(2)}) collective-permute-start(f32[4,128,128]{2,1,0:T(8,128)S(1)} %fusion.56), channel_id=1, source_target_pairs={{8,0},{16,8},{24,16},{32,24},{40,32},{48,40},{56,48},{64,56},{72,6... | collective-permute-start | bytes 786440 | tf_op jit(solution)/shard_map/ppermute | solution.py:13
  119.1 13.9 %copy-start.5 = (bf16[4,512,512]{2,1,0:T(8,128)(2,1)}, bf16[4,512,512]{2,1,0:T(8,128)(2,1)S(1)}, u32[]{:S(2)}) copy-start(bf16[4,512,512]{2,1,0:T(8,128)(2,1)S(1)} %fusion.89) | copy-start | bytes 6291460
  119.1 12.4 %copy-start.9 = (f32[4,128,128]{2,1,0:T(8,128)S(1)}, f32[4,128,128]{2,1,0:T(8,128)}, u32[]{:S(2)}) copy-start(f32[4,128,128]{2,1,0:T(8,128)} %copy-done.8) | copy-start | bytes 786436
  126.8 11.1 %collective-permute-start.6 = (f32[4,128,128]{2,1,0:T(8,128)}, f32[4,128,128]{2,1,0:T(8,128)}, u32[]{:S(2)}, u32[]{:S(2)}) collective-permute-start(f32[4,128,128]{2,1,0:T(8,128)} %collective-permute-done.5), channel_id=1, source_target_pairs={{8,0},{16,8},{24,16},{32,24},{40,32},{48,40},{56,48},{64,56},{72,6... | collective-permute-start | bytes 786440 | tf_op jit(solution)/shard_map/ppermute | solution.py:13
  139.0 17.2 %copy-start.1 = (bf16[512,4,128]{0,2,1:T(8,128)(2,1)S(1)}, bf16[512,4,128]{0,2,1:T(8,128)(2,1)}, u32[]{:S(2)}) copy-start(bf16[512,4,128]{0,2,1:T(8,128)(2,1)} %copy-done) | copy-start | bytes 1572868
  139.0 17.2 %copy-start.7 = (bf16[4,512,512]{2,1,0:T(8,128)(2,1)S(1)}, bf16[4,512,512]{2,1,0:T(8,128)(2,1)}, u32[]{:S(2)}) copy-start(bf16[4,512,512]{2,1,0:T(8,128)(2,1)} %copy-done.6) | copy-start | bytes 6291460
  139.0 17.2 %copy-start.13 = (pred[512,512]{1,0:T(8,128)(4,1)S(1)}, pred[512,512]{1,0:T(8,128)(4,1)}, u32[]{:S(2)}) copy-start(pred[512,512]{1,0:T(8,128)(4,1)} %copy-done.11) | copy-start | bytes 786436
  139.0 12.8 %collective-permute-start.7 = (f32[4,128,128]{2,1,0:T(8,128)S(1)}, f32[4,128,128]{2,1,0:T(8,128)S(1)}, u32[]{:S(2)}, u32[]{:S(2)}) collective-permute-start(f32[4,128,128]{2,1,0:T(8,128)S(1)} %multiply_add_fusion.2), channel_id=1, source_target_pairs={{16,0},{24,8},{32,16},{40,24},{48,32},{56,40},{64,48},{72,56},{80,... | collective-permute-start | bytes 786440 | tf_op jit(solution)/shard_map/ppermute | solution.py:13
  145.6 20.9 %copy-start.3 = (bf16[1,512,512]{1,2,0:T(8,128)(2,1)S(1)}, bf16[1,512,512]{1,2,0:T(8,128)(2,1)}, u32[]{:S(2)}) copy-start(bf16[1,512,512]{1,2,0:T(8,128)(2,1)} %copy-done.2) | copy-start | bytes 1572868
  151.8 14.7 %collective-permute-start.8 = (f32[4,128,128]{2,1,0:T(8,128)S(1)}, f32[4,128,128]{2,1,0:T(8,128)S(1)}, u32[]{:S(2)}, u32[]{:S(2)}) collective-permute-start(f32[4,128,128]{2,1,0:T(8,128)S(1)} %multiply_add_fusion.1), channel_id=1, source_target_pairs={{32,0},{40,8},{48,16},{56,24},{64,32},{72,40},{80,48},{88,56},{96,... | collective-permute-start | bytes 786440 | tf_op jit(solution)/shard_map/ppermute | solution.py:13
  166.5 1.5 copy-start.10
  180.2 139.1 %collective-permute-start.9 = (f32[3,3,512]{2,1,0:T(4,128)S(1)}, f32[3,3,512]{2,1,0:T(4,128)S(1)}, u32[]{:S(2)}, u32[]{:S(2)}) collective-permute-start(f32[3,3,512]{2,1,0:T(4,128)S(1)} %slice.148), channel_id=1, source_target_pairs={{8,0},{16,8},{24,16},{32,24},{40,32},{48,40},{56,48},{64,56},{72,6... | collective-permute-start | bytes 55304 | tf_op jit(solution)/shard_map/ppermute | solution.py:13
Sparse Core Ops, SparseCore 0:
  9.8 37.5 all-gather.1
  103.5 226.5 reduce-scatter.6
  333.4 39.4 reduce-scatter.4

commit v2 on v1

v2 whole, which is shorter than its diff:
```python
import jax
import jax.numpy as jnp
from jax import lax
from jax.experimental import pallas as pl
from jax.experimental.pallas import tpu as pltpu
from jax.sharding import PartitionSpec as P

DH = 128
KW = 4
HEADS = 4
ROWS = 512
WIDTH = 512
DOCS = 8
TOKENS = 16384
NX, NZ, NY = 4, 8, 4
EDGE = 16
BF = jnp.bfloat16
F32 = jnp.float32
MESH = pl.DeviceIdType.MESH
COPIES = 112

LANES = [pl.ds(h * DH, DH) for h in range(HEADS)]


def wrap(value, size):
    return lax.rem(value + size, size)


def lanes_of(head):
    return pl.ds(pl.multiple_of(head * DH, DH), DH)


def dot(a, b, left=1, right=0):
    return lax.dot_general(a, b, (((left,), (right,)), ((), ())), preferred_element_type=F32)


class Links:
    def __init__(self, send_sems, recv_sems):
        self.send_sems, self.recv_sems = send_sems, recv_sems
        self.used, self.pending = 0, []

    def start(self, source, target, device):
        copy = pltpu.make_async_remote_copy(
            src_ref=source,
            dst_ref=target,
            send_sem=self.send_sems.at[self.used],
            recv_sem=self.recv_sems.at[self.used],
            device_id=device,
            device_id_type=MESH,
        )
        self.used += 1
        copy.start()
        self.pending.append(copy)
        return copy

    def drain(self):
        for copy in self.pending:
            copy.wait_send()


def add_into(target, source):
    for tile in range(target.shape[0]):
        target[tile] = (target[tile].astype(F32) + source[tile].astype(F32)).astype(BF)


class Ring:
    def __init__(self, links, n, me, device_of, own, halves, blocks):
        self.links, self.n, self.me = links, n, me
        self.device_of, self.own = device_of, own
        self.halves, self.blocks = halves, blocks
        self.arrivals = {}

    def part(self, way, ref, near):
        half = ref.shape[0] // 2
        first = (way == 0) == near
        return ref.at[pl.ds(0 if first else half, half)]

    def begin(self):
        far = self.n // 2
        for way, sign in ((0, 1), (1, -1)):
            there = self.device_of(wrap(self.me + sign, self.n))
            block = self.own(wrap(self.me + far, self.n))
            self.arrivals[way, 1] = [
                self.links.start(self.part(way, block, True), self.halves.at[way], there)
            ]
        for way, sign in ((0, 1), (1, -1)):
            there = self.device_of(wrap(self.me + sign, self.n))
            block = self.own(wrap(self.me + sign * (far - 1), self.n))
            self.arrivals[way, 2] = [
                self.links.start(
                    self.part(way, block, False),
                    self.part(way, self.blocks.at[way, 0], False),
                    there,
                )
            ]

    def relay(self, step):
        far = self.n // 2
        for way, sign in ((0, 1), (1, -1)):
            there = self.device_of(wrap(self.me + sign, self.n))
            block = self.own(wrap(self.me + sign * (far - step + 1), self.n))
            for copy in self.arrivals[way, step - 1]:
                copy.wait_recv()
            if step == 2:
                mine = self.part(way, block, True)
                add_into(mine, self.halves.at[way])
                landing = self.part(way, self.blocks.at[way, 0], True)
                self.arrivals[way, 2].append(self.links.start(mine, landing, there))
            else:
                add_into(block, self.blocks.at[way, step - 3])
                landing = self.blocks.at[way, step - 2]
                self.arrivals[way, step] = [self.links.start(block, landing, there)]

    def finish(self):
        last = self.n // 2
        for way in (0, 1):
            for copy in self.arrivals[way, last]:
                copy.wait_recv()
        return self.own(self.me), self.blocks.at[0, last - 2], self.blocks.at[1, last - 2]


def kernel(
    docs, proj_hbm, taps, weight_hbm, grad_hbm,
    mixed_out, gproj_out, gtaps_out, gweight_out,
    proj, weight, og, rim, grim,
    mask_back, mask_next, mask_head, mask_tail, allowed,
    qf, kf, val, probs, unit, scale, gunit, normed, normed_t, go, gprobs, gacts,
    fwd_send, fwd_in, fwd_row, fwd_rowin, fwd_out, state,
    bwd_send, bwd_in, bwd_row, bwd_rowin, bwd_out, gstate,
    sib_send, sib_recv, mix, mix_half, mix_block,
    gx, gx_half, gx_block, gx2, gx2_half, gx2_block,
    gz, gz_half, gz_block, gz2, gz2_half, gz2_block,
    tap_part, tap_in, tap_row, tap_rowin,
    local_sems, send_sems, recv_sems,
):
    seq, head = lax.axis_index("seq"), lax.axis_index("head")
    x, z = seq // NZ, lax.rem(seq, NZ)
    y, core = head // 2, lax.rem(head, 2)
    at_x = lambda to: (to * NZ + z, head)
    at_z = lambda to: (x * NZ + to, head)
    at_y = lambda to: (seq, to * 2 + core)
    sibling = (seq, y * 2 + (1 - core))
    token_next = (wrap(seq + 1, NX * NZ), head)
    token_prev = (wrap(seq - 1, NX * NZ), head)
    links = Links(send_sems, recv_sems)

    load_proj = pltpu.make_async_copy(proj_hbm, proj, local_sems.at[0])
    load_grad = pltpu.make_async_copy(grad_hbm, og.at[head], local_sems.at[1])
    load_weight = pltpu.make_async_copy(weight_hbm, weight, local_sems.at[2])
    load_grad.start()
    load_proj.start()
    load_weight.start()

    partners = [sibling, at_y(wrap(y + 1, NY)), at_y(wrap(y - 1, NY)), token_next, token_prev]
    partners += [at_x(wrap(x + k, NX)) for k in range(1, NX)]
    partners += [at_z(wrap(z + k, NZ)) for k in range(1, NZ)]
    barrier = pltpu.get_barrier_semaphore()
    for partner in partners:
        pl.semaphore_signal(barrier, inc=1, device_id=partner, device_id_type=MESH)

    starts = []
    total = jnp.int32(0)
    for i in range(DOCS):
        starts.append(total)
        total = total + docs[i]
    offset = seq * ROWS

    def doc_at(position):
        count = jnp.int32(0)
        for start in starts:
            count = count + jnp.where(start <= position, 1, 0)
        return count

    ends = [doc_at((x * NZ + k) * ROWS - 1) for k in range(NZ + 1)]
    same = lambda a, b: jnp.where(ends[a] == ends[b], jnp.float32(1), jnp.float32(0))

    position = offset + lax.broadcasted_iota(jnp.int32, (ROWS, DH), 0)
    doc_start = jnp.zeros((ROWS, DH), jnp.int32)
    doc_end = jnp.full((ROWS, DH), TOKENS, jnp.int32)
    for i in range(1, DOCS):
        doc_start = jnp.where(starts[i] <= position, starts[i], doc_start)
    for i in range(DOCS - 1, 0, -1):
        doc_end = jnp.where(starts[i] > position, starts[i], doc_end)
    one, zero = jnp.float32(1), jnp.float32(0)
    for j in range(1, KW):
        mask_back[j - 1] = jnp.where(position - j >= doc_start, one, zero)
        mask_next[j - 1] = jnp.where(position + j < doc_end, one, zero)
    mask_head[...] = jnp.where(doc_start < offset, one, zero)
    mask_tail[...] = jnp.where(doc_end > offset + ROWS - 1, one, zero)
    for tile in range(ROWS // DH):
        column = offset + tile * DH + lax.broadcasted_iota(jnp.int32, (ROWS, DH), 1)
        allowed[:, tile * DH : (tile + 1) * DH] = jnp.where(
            (column <= position) & (column >= doc_start), one, zero
        )

    load_grad.wait()
    pl.semaphore_wait(barrier, len(partners))

    half = ROWS // 2
    up, down, across = wrap(y + 1, NY), wrap(y - 1, NY), wrap(y + 2, NY)
    block_of = lambda to: to * 2 + core
    top = lambda to: og.at[block_of(to), pl.ds(0, half)]
    bottom = lambda to: og.at[block_of(to), pl.ds(half, half)]
    whole = lambda to: og.at[block_of(to)]
    up_top = links.start(top(y), top(y), at_y(up))
    down_bottom = links.start(bottom(y), bottom(y), at_y(down))
    up_bottom = links.start(bottom(y), bottom(y), at_y(up))
    down_top = links.start(top(y), top(y), at_y(down))
    load_proj.wait()
    rim_copy = links.start(proj.at[:, pl.ds(ROWS - EDGE, EDGE)], rim, token_next)
    sib_own = links.start(whole(y), whole(y), sibling)

    def activate(stream, acc, rows, lanes):
        act = acc.astype(BF)
        if stream == 2:
            val[rows, lanes] = act
        else:
            wide = act.astype(F32)
            feature = jnp.where(wide > 0, wide + 1.0, jnp.exp(jnp.minimum(wide, 0.0)))
            (qf, kf)[stream][rows, lanes] = feature.astype(BF)

    def convolve(number, _):
        lanes = lanes_of(number)
        for stream in range(3):
            raw = proj[stream, :, lanes].astype(F32)
            acc = taps[stream, 0:1, lanes] * raw
            for j in range(1, KW):
                acc = acc + taps[stream, j : j + 1, lanes] * (
                    pltpu.roll(raw, j, 0) * mask_back[j - 1]
                )
            activate(stream, acc, slice(None), lanes)
        return 0

    lax.fori_loop(0, HEADS, convolve, 0)
    rim_copy.wait_recv()

    def convolve_rim(number, _):
        lanes = lanes_of(number)
        for stream in range(3):
            raw = proj[stream, 0:EDGE, lanes].astype(F32)
            both = jnp.concatenate([rim[stream, :, lanes].astype(F32), raw], axis=0)
            acc = taps[stream, 0:1, lanes] * raw
            for j in range(1, KW):
                acc = acc + taps[stream, j : j + 1, lanes] * (
                    pltpu.roll(both, j, 0)[EDGE:] * mask_back[j - 1, 0:EDGE]
                )
            activate(stream, acc, slice(0, EDGE), lanes)
        return 0

    lax.fori_loop(0, HEADS, convolve_rim, 0)

    def tail_state(number, _):
        lanes = lanes_of(number)
        keys = (kf[:, lanes].astype(F32) * mask_tail[...]).astype(BF)
        local = dot(keys, val[:, lanes], 0, 0)
        fwd_send[pl.ds(2 * number, 2)] = local.astype(BF).reshape(2, DH // 2, DH)
        return 0

    def to_owners(send, landing):
        return [
            links.start(send.at[wrap(z + k, NZ)], landing.at[z], at_z(wrap(z + k, NZ)))
            for k in range(1, NZ)
        ]

    lax.fori_loop(0, HEADS, tail_state, 0)
    fwd_copies = to_owners(fwd_send, fwd_in)
    fwd_in[z] = fwd_send[z]

    up_top.wait_recv()
    pass_top = links.start(top(down), top(down), at_y(up))
    down_bottom.wait_recv()
    pass_bottom = links.start(bottom(up), bottom(up), at_y(down))

    def local_attention(number, _):
        lanes = lanes_of(number)
        for r in range(ROWS // DH):
            rows, width = slice(r * DH, (r + 1) * DH), (r + 1) * DH
            scores = dot(qf[rows, lanes], kf[0:width, lanes], 1, 1)
            kept = (scores * allowed[rows, 0:width]).astype(BF)
            probs[number, rows, 0:width] = kept
            unit[rows, lanes] = dot(kept, val[0:width, lanes])
        return 0

    lax.fori_loop(0, HEADS, local_attention, 0)

    for copy in fwd_copies:
        copy.wait_recv()
    run = jnp.zeros((DH // 2, DH), F32)
    prefix = []
    for k in range(NZ):
        prefix.append(run)
        run = fwd_in[k].astype(F32) + same(k, k + 1) * run
    fwd_row[...] = run.astype(BF)
    row_copy = links.start(fwd_row, fwd_rowin, at_x(wrap(x + 1, NX)))

    load_weight.wait()

    def add_gunit(block, first=False):
        columns = pl.ds(pl.multiple_of(block * WIDTH, WIDTH), WIDTH)

        def tile(r, _):
            rows = pl.ds(pl.multiple_of(r * 256, 256), 256)
            part = dot(og[block, rows, :], weight[:, columns], 1, 1)
            gunit[rows, :] = part if first else gunit[rows, :] + part
            return 0

        lax.fori_loop(0, ROWS // 256, tile, 0)

    add_gunit(block_of(y), True)
    row_copy.wait_recv()
    carried = fwd_rowin[...].astype(F32)
    for k in range(NZ):
        fwd_out[k] = (prefix[k] + same(k, 0) * carried).astype(BF)
    out_copies = to_owners(fwd_out, state)
    state[z] = fwd_out[z]

    other = lambda to: to * 2 + (1 - core)
    sib_own.wait_recv()
    add_gunit(other(y))
    up_bottom.wait_recv()
    sib_down = links.start(whole(down), whole(down), sibling)
    down_top.wait_recv()
    sib_up = links.start(whole(up), whole(up), sibling)
    add_gunit(block_of(down))
    add_gunit(block_of(up))

    for copy in out_copies:
        copy.wait_recv()

    def finish_attention(number, _):
        lanes = lanes_of(number)
        carried_in = state[pl.ds(2 * number, 2)].reshape(DH, DH)
        attn = unit[:, lanes] + mask_head[...] * dot(qf[:, lanes], carried_in)
        factor = lax.rsqrt(jnp.mean(attn * attn, axis=1, keepdims=True) + 1e-06)
        scaled = attn * factor
        unit[:, lanes] = scaled
        scale[number] = jnp.broadcast_to(factor, (ROWS, DH))
        normed[:, lanes] = scaled.astype(BF)
        normed_t[lanes_of(number), :] = scaled.T.astype(BF)
        return 0

    lax.fori_loop(0, HEADS, finish_attention, 0)

    sib_down.wait_recv()
    add_gunit(other(down))
    sib_up.wait_recv()
    add_gunit(other(up))
    pass_top.wait_recv()
    pass_bottom.wait_recv()
    sib_across = links.start(whole(across), whole(across), sibling)
    add_gunit(block_of(across))
    sib_across.wait_recv()
    add_gunit(other(across))

    def weight_x(block, _):
        part = dot(normed_t[0:half, :], og[block]).astype(BF)
        for j in range(4):
            gx[block * 4 + j] = part[:, j * DH : (j + 1) * DH]
        return 0

    def weight_z(block, _):
        part = dot(normed_t[half:ROWS, :], og[block]).astype(BF)
        for j in range(4):
            gz[(lax.rem(block, 2) * 4 + j) * NX + block // 2] = part[:, j * DH : (j + 1) * DH]
        return 0

    ring_x = Ring(links, NX, x, at_x, lambda to: gx.at[pl.ds(to * NZ, NZ)], gx_half, gx_block)
    ring_z = Ring(links, NZ, z, at_z, lambda to: gz.at[pl.ds(to * NX, NX)], gz_half, gz_block)
    lax.fori_loop(0, 8, weight_x, 0)
    ring_x.begin()
    lax.fori_loop(0, 8, weight_z, 0)
    ring_z.begin()

    def grad_attn(number, _):
        lanes = lanes_of(number)
        given, scaled = gunit[:, lanes], unit[:, lanes]
        inner = jnp.mean(given * scaled, axis=1, keepdims=True)
        grad = (scale[number] * (given - scaled * inner)).astype(BF)
        go[:, lanes] = grad
        queries = (qf[:, lanes].astype(F32) * mask_head[...]).astype(BF)
        local = dot(queries, grad, 0, 0)
        bwd_send[pl.ds(2 * number, 2)] = local.astype(BF).reshape(2, DH // 2, DH)
        return 0

    lax.fori_loop(0, HEADS, grad_attn, 0)
    bwd_copies = to_owners(bwd_send, bwd_in)
    bwd_in[z] = bwd_send[z]

    ring_y = Ring(links, NY, y, at_y, lambda to: mix.at[to], mix_half, mix_block)
    order = [across, up, down, y]

    def project(block, put):
        columns = pl.ds(pl.multiple_of(block * WIDTH, WIDTH), WIDTH)

        def tile(r, _):
            rows = pl.ds(pl.multiple_of(r * half, half), half)
            put(r, dot(normed[rows, :], weight[:, columns]))
            return 0

        lax.fori_loop(0, 2, tile, 0)

    sib_copies = []
    for k, to in enumerate(order):

        def put_sib(r, part, k=k):
            sib_send[k, r] = part.astype(BF)

        project(other(to), put_sib)
        sib_copies.append(links.start(sib_send.at[k], sib_recv.at[k], sibling))

    def put_own(k, to):
        sib_copies[k].wait_recv()

        def put(r, part):
            mix[to, r] = (part + sib_recv[k, r].astype(F32)).astype(BF)

        project(block_of(to), put)

    for k, to in enumerate(order[:3]):
        put_own(k, to)
    ring_y.begin()
    put_own(3, y)

    ring_z.relay(2)

    for copy in bwd_copies:
        copy.wait_recv()
    run = jnp.zeros((DH // 2, DH), F32)
    suffix = [None] * NZ
    for k in range(NZ - 1, -1, -1):
        suffix[k] = run
        run = bwd_in[k].astype(F32) + same(k, k + 1) * run
    bwd_row[...] = run.astype(BF)
    back_copy = links.start(bwd_row, bwd_rowin, at_x(wrap(x - 1, NX)))

    def backward_local(number, _):
        lanes = lanes_of(number)
        for r in range(ROWS // DH):
            rows, width = slice(r * DH, (r + 1) * DH), (r + 1) * DH
            scores = dot(go[rows, lanes], val[0:width, lanes], 1, 1)
            kept = (scores * allowed[rows, 0:width]).astype(BF)
            gprobs[rows, 0:width] = kept
            gacts[0, rows, lanes] = dot(kept, kf[0:width, lanes])
        for r in range(ROWS // DH):
            rows, below = slice(r * DH, (r + 1) * DH), slice(r * DH, ROWS)
            gacts[1, rows, lanes] = dot(gprobs[below, rows], qf[below, lanes], 0, 0)
            gacts[2, rows, lanes] = dot(probs[number, below, rows], go[below, lanes], 0, 0)
        return 0

    back_copy.wait_recv()
    carried = bwd_rowin[...].astype(F32)
    for k in range(NZ):
        bwd_out[k] = (suffix[k] + same(k + 1, NZ) * carried).astype(BF)
    gout_copies = to_owners(bwd_out, gstate)
    gstate[z] = bwd_out[z]

    ring_x.relay(2)
    lax.fori_loop(0, HEADS, backward_local, 0)
    ring_z.relay(3)
    ring_y.relay(2)

    for copy in gout_copies:
        copy.wait_recv()

    def backward_state(number, _):
        lanes = lanes_of(number)
        carried_in = state[pl.ds(2 * number, 2)].reshape(DH, DH)
        carried_out = gstate[pl.ds(2 * number, 2)].reshape(DH, DH)
        queries, keys, values = qf[:, lanes], kf[:, lanes], val[:, lanes]
        slope = jnp.minimum(queries.astype(F32), 1.0)
        back = mask_head[...] * dot(go[:, lanes], carried_in, 1, 1)
        gacts[0, :, lanes] = (gacts[0, :, lanes] + back) * slope
        slope = jnp.minimum(keys.astype(F32), 1.0)
        back = mask_tail[...] * dot(values, carried_out, 1, 1)
        gacts[1, :, lanes] = (gacts[1, :, lanes] + back) * slope
        back = mask_tail[...] * dot(keys, carried_out)
        gacts[2, :, lanes] = gacts[2, :, lanes] + back
        return 0

    lax.fori_loop(0, HEADS, backward_state, 0)
    grim_copy = links.start(gacts.at[:, pl.ds(0, 8)], grim, token_prev)
    ring_z.relay(4)

    def unconvolve(number, _):
        lanes = lanes_of(number)
        for stream in range(3):
            grad = gacts[stream, :, lanes]
            raw = proj[stream, :, lanes].astype(F32)
            both = jnp.concatenate([rim[stream, :, lanes].astype(F32), raw], axis=0)
            acc = taps[stream, 0:1, lanes] * grad
            row = 4 * stream
            tap_part[row : row + 1, lanes] = jnp.sum(grad * raw, axis=0, keepdims=True)
            for j in range(1, KW):
                acc = acc + taps[stream, j : j + 1, lanes] * (
                    pltpu.roll(grad, ROWS - j, 0) * mask_next[j - 1]
                )
                lagged = pltpu.roll(both, j, 0)[EDGE:]
                tap_part[row + j : row + j + 1, lanes] = jnp.sum(
                    grad * mask_back[j - 1] * lagged, axis=0, keepdims=True
                )
            gproj_out[stream, :, lanes] = acc.astype(BF)
        return 0

    tap_part[12:16, :] = jnp.zeros((4, WIDTH), F32)
    lax.fori_loop(0, HEADS, unconvolve, 0)
    tap_copies = [
        links.start(tap_part, tap_in.at[z], at_z(wrap(z + k, NZ))) for k in range(1, NZ)
    ]
    tap_in[z] = tap_part[...]

    grim_copy.wait_recv()

    def unconvolve_rim(number, _):
        lanes = lanes_of(number)
        for stream in range(3):
            grad = gacts[stream, ROWS - EDGE : ROWS, lanes]
            both = jnp.concatenate([grad, grim[stream, :, lanes]], axis=0)
            acc = taps[stream, 0:1, lanes] * grad
            for j in range(1, KW):
                acc = acc + taps[stream, j : j + 1, lanes] * (
                    pltpu.roll(both, EDGE + 8 - j, 0)[0:EDGE]
                    * mask_next[j - 1, ROWS - EDGE : ROWS]
                )
            gproj_out[stream, ROWS - EDGE : ROWS, lanes] = acc.astype(BF)
        return 0

    lax.fori_loop(0, HEADS, unconvolve_rim, 0)

    for copy in tap_copies:
        copy.wait_recv()
    summed = tap_in[0]
    for k in range(1, NZ):
        summed = summed + tap_in[k]
    tap_row[...] = summed
    row_copies = [
        links.start(tap_row, tap_rowin.at[x], at_x(wrap(x + k, NX))) for k in range(1, NX)
    ]
    tap_rowin[x] = tap_row[...]

    ring_x2 = Ring(links, NZ, z, at_z, lambda to: gx2.at[to], gx2_half, gx2_block)
    ring_z2 = Ring(links, NX, x, at_x, lambda to: gz2.at[to], gz2_half, gz2_block)

    def second(ring, target):
        own, first, last = ring.finish()
        for k in range(own.shape[0]):
            value = own[k].astype(F32) + first[k].astype(F32) + last[k].astype(F32)
            target[k] = value.astype(BF).reshape(2, DH, DH)

    second(ring_x, gx2)
    ring_x2.begin()
    second(ring_z, gz2)
    ring_z2.begin()
    ring_x2.relay(2)
    ring_z2.relay(2)
    ring_x2.relay(3)

    own, first, last = ring_y.finish()
    for r in range(2):
        value = own[r].astype(F32) + first[r].astype(F32) + last[r].astype(F32)
        mixed_out[r * half : (r + 1) * half, :] = value.astype(BF)
    ring_x2.relay(4)

    for copy in row_copies:
        copy.wait_recv()
    summed = tap_rowin[0]
    for k in range(1, NX):
        summed = summed + tap_rowin[k]
    for stream in range(3):
        gtaps_out[stream] = summed[4 * stream : 4 * stream + 4, :]

    for ring, base in ((ring_z2, half), (ring_x2, 0)):
        own, first, last = ring.finish()
        for r in range(2):
            value = own[r].astype(F32) + first[r].astype(F32) + last[r].astype(F32)
            gweight_out[base + r * DH : base + (r + 1) * DH, :] = value
    links.drain()


def body(projected, conv_weight, out_weight, out_grad, doc_lengths):
    vm = lambda *shape: pltpu.VMEM(shape, BF)
    vf = lambda *shape: pltpu.VMEM(shape, F32)
    piece = (DH // 2, DH)
    hops = lambda n, m, *tile: [vm(2, m // 2, *tile), vm(2, n // 2 - 1, m, *tile)]
    carry = [vm(NZ, *piece), vm(NZ, *piece), vm(*piece), vm(*piece), vm(NZ, *piece), vm(NZ, *piece)]
    scratch = [
        vm(3, ROWS, WIDTH), vm(WIDTH, 8 * WIDTH), vm(8, ROWS, WIDTH), vm(3, EDGE, WIDTH), vf(3, 8, WIDTH),
        vf(3, ROWS, DH), vf(3, ROWS, DH), vf(ROWS, DH), vf(ROWS, DH), vf(ROWS, ROWS),
        vm(ROWS, WIDTH), vm(ROWS, WIDTH), vm(ROWS, WIDTH), vm(HEADS, ROWS, ROWS), vf(ROWS, WIDTH),
        vf(HEADS, ROWS, DH), vf(ROWS, WIDTH), vm(ROWS, WIDTH), vm(WIDTH, ROWS), vm(ROWS, WIDTH),
        vm(ROWS, ROWS), vf(3, ROWS, WIDTH),
        *carry, *carry,
        vm(4, 2, 256, WIDTH), vm(4, 2, 256, WIDTH), vm(4, 2, 256, WIDTH), *hops(NY, 2, 256, WIDTH),
        vm(32, 256, DH), *hops(NX, NZ, 256, DH), vm(NZ, 2, DH, DH), *hops(NZ, 2, DH, DH),
        vm(32, 256, DH), *hops(NZ, NX, 256, DH), vm(NX, 2, DH, DH), *hops(NX, 2, DH, DH),
        vf(16, WIDTH), vf(NZ, 16, WIDTH), vf(16, WIDTH), vf(NX, 16, WIDTH),
        pltpu.SemaphoreType.DMA((3,)), pltpu.SemaphoreType.DMA((COPIES,)), pltpu.SemaphoreType.DMA((COPIES,)),
    ]
    vmem = pl.BlockSpec(memory_space=pltpu.VMEM)
    outside = pl.BlockSpec(memory_space=pl.ANY)
    mixed, grad_projected, grad_conv, grad_out_weight = pl.pallas_call(
        kernel,
        out_shape=(
            jax.ShapeDtypeStruct((ROWS, WIDTH), BF),
            jax.ShapeDtypeStruct((3, ROWS, WIDTH), BF),
            jax.ShapeDtypeStruct((3, KW, WIDTH), F32),
            jax.ShapeDtypeStruct((WIDTH, DH), F32),
        ),
        in_specs=[pl.BlockSpec(memory_space=pltpu.SMEM), outside, vmem, outside, outside],
        out_specs=(vmem, vmem, vmem, vmem),
        scratch_shapes=scratch,
        compiler_params=pltpu.CompilerParams(
            collective_id=0, has_side_effects=True, vmem_limit_bytes=58 * 2**20
        ),
        cost_estimate=pl.CostEstimate(
            flops=8 * 10**9, bytes_accessed=10**7, transcendentals=10**6
        ),
    )(doc_lengths, projected, conv_weight, out_weight, out_grad)
    return mixed, grad_projected, grad_conv, grad_out_weight


def solution(mesh):
    return jax.shard_map(
        body,
        mesh=mesh,
        in_specs=(
            P(None, "seq", "head"),
            P(None, None, "head"),
            P("head", None),
            P("seq", "head"),
            P(),
        ),
        out_specs=(
            P("seq", "head"),
            P(None, "seq", "head"),
            P(None, None, "head"),
            P("head", "seq"),
        ),
        check_vma=False,
    )
```

time: 381 us -> 106 us (0.28)
  blocking collectives: 122 us -> 0 us
  waiting for transfers between devices: 110 us -> 0 us
  Pallas kernels: 0 us -> 99.7 us
  starting transfers between devices: 49.3 us -> 0 us
  matrix products: 34.4 us -> 0 us
  other arithmetic: 23.7 us -> 0 us
  between operations: 21.7 us -> 0.64 us
  local copies, waits for them, and re-layouts: 18.7 us -> 5.88 us
    psum x1 -> x0, blocking collectives: 122 us -> none  [body(): grad_conv = lax.psum(jnp.stack(tap_sums, axis=1), 'seq')]
    pallas_call x0 -> x1, Pallas kernels: none -> 99.7 us  [body(): pl.pallas_call(kernel, out_shape=(jax.ShapeDtypeStruct((ROWS, WIDTH), BF)...]
    ppermute x10 -> x0, waiting for transfers between devices: 60.7 us -> none  [from_behind(): return lax.ppermute(array, axis, pairs)]
    ppermute x10 -> x0, starting transfers between devices: 49 us -> none  [from_behind(): return lax.ppermute(array, axis, pairs)]
    reduce_scatter x1 -> x0, waiting for transfers between devices: 41.1 us -> none  [body(): lax.psum_scatter(lax.dot_general(columns, normed, (((0,), (1,)), ((), ())...]
    dot_general x15 -> x0, matrix products: 34.4 us -> none  [the longest x1 7.17 us: body(): lax.dot_general(full_grad, out_weight, (((1,), (1,)), ((), ())), preferre...]
    convert_element_type x4 -> x0, other arithmetic: 10.7 us -> none  [the longest x1 5.03 us: body(): acts = conv_sum.astype(jnp.bfloat16)]
    unnamed x4 -> x0, waiting for transfers between devices: 8.08 us -> none
  transfers between devices with their start and end apart: 13 -> 0, of which waited for: 11 -> 0; matrix products, arithmetic and copies ran while one was open for 15% -> 0% of each run, Pallas kernels for 0% -> 0%
where the time goes in v2:
time: 106 us
  Pallas kernels  99.7 us (94%)
  local copies, waits for them, and re-layouts  5.88 us (6%)
    pallas_call x1, Pallas kernels, body(): pl.pallas_call(kernel, out_shape=(jax.ShapeDtypeStruct((ROWS, WIDTH), BF)...  99.7 us
    unnamed x8, local copies, waits for them, and re-layouts  5.88 us

profile of v2, /device:TPU:6, one launch (start us, length us, event | category | flops | bytes accessed | tf_op | source)
XLA Modules:
  0.0 106.2 jit_solution(1795061363190301042)
XLA Ops:
  0.6 99.7 %shard_map.84 = (bf16[512,512]{1,0:T(8,128)(2,1)}, bf16[3,512,512]{2,1,0:T(8,128)(2,1)}, f32[3,4,512]{2,1,0:T(4,128)}, f32[512,128]{1,0:T(8,128)}) custom-call(s32[8]{0:T(128)} %docs.1, bf16[3,512,512]{2,1,0:T(8,128)(2,1)} %proj_hbm.1, f32[3,4,512]{2,1,0:T(4,128)} %taps.1, bf16[512,4096]{1,0:T(8,128)(2,1)} %weight_hbm.1, bf16[512,512]{1,0:T(8,128)(2,1)} %grad_hbm.1), custom_call_target="tpu_custom_call" | custom-call | flops 8000000000 | bytes 10000000 | tf_op jit(solution)/shard_map/pallas_call | solution.py:600
  100.3 1.9 %copy.13 = bf16[512,512]{1,0:T(8,128)(2,1)} copy(bf16[512,512]{1,0:T(8,128)(2,1)} %get-tuple-element.8) | data formatting | bytes 1048576
  102.2 0.0 copy-start.1
  102.2 0.0 copy-start
  102.2 2.7 %copy.14 = bf16[3,512,512]{2,1,0:T(8,128)(2,1)} copy(bf16[3,512,512]{2,1,0:T(8,128)(2,1)} %get-tuple-element.9) | data formatting | bytes 3145728
  104.9 0.0 copy-done.1
  104.9 0.6 copy.15
  105.5 0.0 copy-done
  105.5 0.7 copy.16
Async XLA Ops:
  102.2 2.7 %copy-start.1 = (f32[3,4,512]{2,1,0:T(4,128)S(1)}, f32[3,4,512]{2,1,0:T(4,128)}, u32[]{:S(2)}) copy-start(f32[3,4,512]{2,1,0:T(4,128)} %get-tuple-element.10) | copy-start | bytes 73732
  102.2 3.3 %copy-start = (f32[512,128]{1,0:T(8,128)S(1)}, f32[512,128]{1,0:T(8,128)}, u32[]{:S(2)}) copy-start(f32[512,128]{1,0:T(8,128)} %get-tuple-element.11) | copy-start | bytes 786436

commit v3 on v2

--- a/solution.py
+++ b/solution.py
@@ -17,9 +17,9 @@
 BF = jnp.bfloat16
 F32 = jnp.float32
 MESH = pl.DeviceIdType.MESH
-COPIES = 112
-
-LANES = [pl.ds(h * DH, DH) for h in range(HEADS)]
+COPIES = 144
+ZROWS = 256
+XROWS = WIDTH - ZROWS
 
 
 def wrap(value, size):
@@ -130,7 +130,7 @@
     sib_send, sib_recv, mix, mix_half, mix_block,
     gx, gx_half, gx_block, gx2, gx2_half, gx2_block,
     gz, gz_half, gz_block, gz2, gz2_half, gz2_block,
-    tap_part, tap_in, tap_row, tap_rowin,
+    tap_part, tap_send, tap_in, tap_row, tap_rowin,
     local_sems, send_sems, recv_sems,
 ):
     seq, head = lax.axis_index("seq"), lax.axis_index("head")
@@ -144,19 +144,33 @@
     token_prev = (wrap(seq - 1, NX * NZ), head)
     links = Links(send_sems, recv_sems)
 
-    load_proj = pltpu.make_async_copy(proj_hbm, proj, local_sems.at[0])
-    load_grad = pltpu.make_async_copy(grad_hbm, og.at[head], local_sems.at[1])
-    load_weight = pltpu.make_async_copy(weight_hbm, weight, local_sems.at[2])
-    load_grad.start()
-    load_proj.start()
-    load_weight.start()
-
     partners = [sibling, at_y(wrap(y + 1, NY)), at_y(wrap(y - 1, NY)), token_next, token_prev]
     partners += [at_x(wrap(x + k, NX)) for k in range(1, NX)]
     partners += [at_z(wrap(z + k, NZ)) for k in range(1, NZ)]
     barrier = pltpu.get_barrier_semaphore()
     for partner in partners:
         pl.semaphore_signal(barrier, inc=1, device_id=partner, device_id_type=MESH)
+    load_proj = pltpu.make_async_copy(proj_hbm, proj, local_sems.at[0])
+    load_grad = pltpu.make_async_copy(grad_hbm, og.at[head], local_sems.at[1])
+    load_weight = pltpu.make_async_copy(weight_hbm, weight, local_sems.at[2])
+    load_proj.start()
+    load_grad.start()
+    load_weight.start()
+    pl.semaphore_wait(barrier, len(partners))
+
+    half = ROWS // 2
+    up, down, across = wrap(y + 1, NY), wrap(y - 1, NY), wrap(y + 2, NY)
+    block_of = lambda to: to * 2 + core
+    upper, lower = pl.ds(0, half), pl.ds(half, half)
+    top = lambda to: og.at[block_of(to), upper]
+    bottom = lambda to: og.at[block_of(to), lower]
+    whole = lambda to: og.at[block_of(to)]
+    up_top = links.start(grad_hbm.at[upper], top(y), at_y(up))
+    down_bottom = links.start(grad_hbm.at[lower], bottom(y), at_y(down))
+    rim_copy = links.start(proj_hbm.at[:, pl.ds(ROWS - EDGE, EDGE)], rim, token_next)
+    up_bottom = links.start(grad_hbm.at[lower], bottom(y), at_y(up))
+    down_top = links.start(grad_hbm.at[upper], top(y), at_y(down))
+    sib_own = links.start(grad_hbm, whole(y), sibling)
 
     starts = []
     total = jnp.int32(0)
@@ -193,22 +207,7 @@
             (column <= position) & (column >= doc_start), one, zero
         )
 
-    load_grad.wait()
-    pl.semaphore_wait(barrier, len(partners))
-
-    half = ROWS // 2
-    up, down, across = wrap(y + 1, NY), wrap(y - 1, NY), wrap(y + 2, NY)
-    block_of = lambda to: to * 2 + core
-    top = lambda to: og.at[block_of(to), pl.ds(0, half)]
-    bottom = lambda to: og.at[block_of(to), pl.ds(half, half)]
-    whole = lambda to: og.at[block_of(to)]
-    up_top = links.start(top(y), top(y), at_y(up))
-    down_bottom = links.start(bottom(y), bottom(y), at_y(down))
-    up_bottom = links.start(bottom(y), bottom(y), at_y(up))
-    down_top = links.start(top(y), top(y), at_y(down))
     load_proj.wait()
-    rim_copy = links.start(proj.at[:, pl.ds(ROWS - EDGE, EDGE)], rim, token_next)
-    sib_own = links.start(whole(y), whole(y), sibling)
 
     def activate(stream, acc, rows, lanes):
         act = acc.astype(BF)
@@ -293,6 +292,7 @@
     fwd_row[...] = run.astype(BF)
     row_copy = links.start(fwd_row, fwd_rowin, at_x(wrap(x + 1, NX)))
 
+    load_grad.wait()
     load_weight.wait()
 
     def add_gunit(block, first=False):
@@ -341,6 +341,28 @@
 
     lax.fori_loop(0, HEADS, finish_attention, 0)
 
+    def weight_band(band):
+        def one_block(which, _):
+            block = band * 2 + which
+            part = dot(normed_t[0:XROWS, :], og[block]).astype(BF)
+            for j in range(4):
+                gx[block * 4 + j] = part[:, j * DH : (j + 1) * DH]
+            part = dot(normed_t[XROWS:WIDTH, :], og[block]).astype(BF)
+            for j in range(4):
+                tile = part[:, j * DH : (j + 1) * DH]
+                gz[band, which * 4 + j] = tile.reshape(2, ZROWS // 2, DH)
+            return 0
+
+        lax.fori_loop(0, 2, one_block, 0)
+
+    ring_x = Ring(links, NX, x, at_x, lambda to: gx.at[pl.ds(to * NZ, NZ)], gx_half, gx_block)
+    order = [y, down, up, across]
+    rings_z = [
+        Ring(links, NZ, z, at_z, lambda to, b=b: gz.at[b, to], gz_half.at[k], gz_block.at[k])
+        for k, b in enumerate(order)
+    ]
+    weight_band(y)
+    rings_z[0].begin()
     sib_down.wait_recv()
     add_gunit(other(down))
     sib_up.wait_recv()
@@ -348,28 +370,16 @@
     pass_top.wait_recv()
     pass_bottom.wait_recv()
     sib_across = links.start(whole(across), whole(across), sibling)
+    weight_band(down)
+    rings_z[1].begin()
+    weight_band(up)
+    rings_z[2].begin()
     add_gunit(block_of(across))
     sib_across.wait_recv()
     add_gunit(other(across))
-
-    def weight_x(block, _):
-        part = dot(normed_t[0:half, :], og[block]).astype(BF)
-        for j in range(4):
-            gx[block * 4 + j] = part[:, j * DH : (j + 1) * DH]
-        return 0
-
-    def weight_z(block, _):
-        part = dot(normed_t[half:ROWS, :], og[block]).astype(BF)
-        for j in range(4):
-            gz[(lax.rem(block, 2) * 4 + j) * NX + block // 2] = part[:, j * DH : (j + 1) * DH]
-        return 0
-
-    ring_x = Ring(links, NX, x, at_x, lambda to: gx.at[pl.ds(to * NZ, NZ)], gx_half, gx_block)
-    ring_z = Ring(links, NZ, z, at_z, lambda to: gz.at[pl.ds(to * NX, NX)], gz_half, gz_block)
-    lax.fori_loop(0, 8, weight_x, 0)
+    weight_band(across)
     ring_x.begin()
-    lax.fori_loop(0, 8, weight_z, 0)
-    ring_z.begin()
+    rings_z[3].begin()
 
     def grad_attn(number, _):
         lanes = lanes_of(number)
@@ -385,9 +395,10 @@
     lax.fori_loop(0, HEADS, grad_attn, 0)
     bwd_copies = to_owners(bwd_send, bwd_in)
     bwd_in[z] = bwd_send[z]
+    rings_z[0].relay(2)
 
     ring_y = Ring(links, NY, y, at_y, lambda to: mix.at[to], mix_half, mix_block)
-    order = [across, up, down, y]
+    outward = [across, up, down]
 
     def project(block, put):
         columns = pl.ds(pl.multiple_of(block * WIDTH, WIDTH), WIDTH)
@@ -400,7 +411,7 @@
         lax.fori_loop(0, 2, tile, 0)
 
     sib_copies = []
-    for k, to in enumerate(order):
+    for k, to in enumerate(outward + [y]):
 
         def put_sib(r, part, k=k):
             sib_send[k, r] = part.astype(BF)
@@ -416,12 +427,9 @@
 
         project(block_of(to), put)
 
-    for k, to in enumerate(order[:3]):
-        put_own(k, to)
-    ring_y.begin()
-    put_own(3, y)
-
-    ring_z.relay(2)
+    rings_z[1].relay(2)
+    rings_z[2].relay(2)
+    rings_z[0].relay(3)
 
     for copy in bwd_copies:
         copy.wait_recv()
@@ -432,6 +440,15 @@
         run = bwd_in[k].astype(F32) + same(k, k + 1) * run
     bwd_row[...] = run.astype(BF)
     back_copy = links.start(bwd_row, bwd_rowin, at_x(wrap(x - 1, NX)))
+
+    for k, to in enumerate(outward):
+        put_own(k, to)
+    ring_y.begin()
+    rings_z[3].relay(2)
+    rings_z[1].relay(3)
+    rings_z[2].relay(3)
+    rings_z[0].relay(4)
+    ring_x.relay(2)
 
     def backward_local(number, _):
         lanes = lanes_of(number)
@@ -454,10 +471,11 @@
     gout_copies = to_owners(bwd_out, gstate)
     gstate[z] = bwd_out[z]
 
-    ring_x.relay(2)
     lax.fori_loop(0, HEADS, backward_local, 0)
-    ring_z.relay(3)
-    ring_y.relay(2)
+    rings_z[3].relay(3)
+    rings_z[1].relay(4)
+    rings_z[2].relay(4)
+    put_own(3, y)
 
     for copy in gout_copies:
         copy.wait_recv()
@@ -479,7 +497,8 @@
 
     lax.fori_loop(0, HEADS, backward_state, 0)
     grim_copy = links.start(gacts.at[:, pl.ds(0, 8)], grim, token_prev)
-    ring_z.relay(4)
+    ring_y.relay(2)
+    rings_z[3].relay(4)
 
     def unconvolve(number, _):
         lanes = lanes_of(number)
@@ -503,10 +522,11 @@
 
     tap_part[12:16, :] = jnp.zeros((4, WIDTH), F32)
     lax.fori_loop(0, HEADS, unconvolve, 0)
+    tap_send[...] = tap_part[...].astype(BF)
     tap_copies = [
-        links.start(tap_part, tap_in.at[z], at_z(wrap(z + k, NZ))) for k in range(1, NZ)
+        links.start(tap_send, tap_in.at[z], at_z(wrap(z + k, NZ))) for k in range(1, NZ)
     ]
-    tap_in[z] = tap_part[...]
+    tap_in[z] = tap_send[...]
 
     grim_copy.wait_recv()
 
@@ -526,39 +546,39 @@
 
     lax.fori_loop(0, HEADS, unconvolve_rim, 0)
 
+    ring_x2 = Ring(links, NZ, z, at_z, lambda to: gx2.at[to], gx2_half, gx2_block)
+    ring_z2 = Ring(links, NX, x, at_x, lambda to: gz2.at[to], gz2_half, gz2_block)
+
+    for ring, band in zip(rings_z, order):
+        own, first, last = ring.finish()
+        for r in range(2):
+            value = own[r].astype(F32) + first[r].astype(F32) + last[r].astype(F32)
+            gz2[band, r] = value.astype(BF)
+    ring_z2.begin()
+    own, first, last = ring_x.finish()
+    for k in range(NZ):
+        value = own[k].astype(F32) + first[k].astype(F32) + last[k].astype(F32)
+        gx2[k] = value.astype(BF).reshape(2, XROWS // 2, DH)
+    ring_x2.begin()
+    ring_z2.relay(2)
+
     for copy in tap_copies:
         copy.wait_recv()
-    summed = tap_in[0]
+    summed = tap_in[0].astype(F32)
     for k in range(1, NZ):
-        summed = summed + tap_in[k]
+        summed = summed + tap_in[k].astype(F32)
     tap_row[...] = summed
     row_copies = [
         links.start(tap_row, tap_rowin.at[x], at_x(wrap(x + k, NX))) for k in range(1, NX)
     ]
     tap_rowin[x] = tap_row[...]
-
-    ring_x2 = Ring(links, NZ, z, at_z, lambda to: gx2.at[to], gx2_half, gx2_block)
-    ring_z2 = Ring(links, NX, x, at_x, lambda to: gz2.at[to], gz2_half, gz2_block)
-
-    def second(ring, target):
-        own, first, last = ring.finish()
-        for k in range(own.shape[0]):
-            value = own[k].astype(F32) + first[k].astype(F32) + last[k].astype(F32)
-            target[k] = value.astype(BF).reshape(2, DH, DH)
-
-    second(ring_x, gx2)
-    ring_x2.begin()
-    second(ring_z, gz2)
-    ring_z2.begin()
     ring_x2.relay(2)
-    ring_z2.relay(2)
-    ring_x2.relay(3)
 
     own, first, last = ring_y.finish()
     for r in range(2):
         value = own[r].astype(F32) + first[r].astype(F32) + last[r].astype(F32)
         mixed_out[r * half : (r + 1) * half, :] = value.astype(BF)
-    ring_x2.relay(4)
+    ring_x2.relay(3)
 
     for copy in row_copies:
         copy.wait_recv()
@@ -567,13 +587,26 @@
         summed = summed + tap_rowin[k]
     for stream in range(3):
         gtaps_out[stream] = summed[4 * stream : 4 * stream + 4, :]
-
-    for ring, base in ((ring_z2, half), (ring_x2, 0)):
+    ring_x2.relay(4)
+
+    for ring, base, count in ((ring_z2, XROWS, ZROWS // 2), (ring_x2, 0, XROWS // 2)):
         own, first, last = ring.finish()
         for r in range(2):
             value = own[r].astype(F32) + first[r].astype(F32) + last[r].astype(F32)
-            gweight_out[base + r * DH : base + (r + 1) * DH, :] = value
+            gweight_out[base + r * count : base + (r + 1) * count, :] = value
     links.drain()
+
+
+def hand_over(*refs):
+    sources, targets, sems = refs[:4], refs[4:8], refs[8]
+    copies = [
+        pltpu.make_async_copy(source, target, sems.at[k])
+        for k, (source, target) in enumerate(zip(sources, targets))
+    ]
+    for copy in copies:
+        copy.start()
+    for copy in copies:
+        copy.wait()
 
 
 def body(projected, conv_weight, out_weight, out_grad, doc_lengths):
@@ -590,23 +623,26 @@
         vm(ROWS, ROWS), vf(3, ROWS, WIDTH),
         *carry, *carry,
         vm(4, 2, 256, WIDTH), vm(4, 2, 256, WIDTH), vm(4, 2, 256, WIDTH), *hops(NY, 2, 256, WIDTH),
-        vm(32, 256, DH), *hops(NX, NZ, 256, DH), vm(NZ, 2, DH, DH), *hops(NZ, 2, DH, DH),
-        vm(32, 256, DH), *hops(NZ, NX, 256, DH), vm(NX, 2, DH, DH), *hops(NX, 2, DH, DH),
-        vf(16, WIDTH), vf(NZ, 16, WIDTH), vf(16, WIDTH), vf(NX, 16, WIDTH),
+        vm(32, XROWS, DH), *hops(NX, NZ, XROWS, DH),
+        vm(NZ, 2, XROWS // 2, DH), *hops(NZ, 2, XROWS // 2, DH),
+        vm(NX, NZ, 2, ZROWS // 2, DH), vm(4, 2, 1, ZROWS // 2, DH), vm(4, 2, 3, 2, ZROWS // 2, DH),
+        vm(NX, 2, ZROWS // 2, DH), *hops(NX, 2, ZROWS // 2, DH),
+        vf(16, WIDTH), vm(16, WIDTH), vm(NZ, 16, WIDTH), vf(16, WIDTH), vf(NX, 16, WIDTH),
         pltpu.SemaphoreType.DMA((3,)), pltpu.SemaphoreType.DMA((COPIES,)), pltpu.SemaphoreType.DMA((COPIES,)),
     ]
     vmem = pl.BlockSpec(memory_space=pltpu.VMEM)
     outside = pl.BlockSpec(memory_space=pl.ANY)
-    mixed, grad_projected, grad_conv, grad_out_weight = pl.pallas_call(
+    shapes = (
+        jax.ShapeDtypeStruct((ROWS, WIDTH), BF),
+        jax.ShapeDtypeStruct((3, ROWS, WIDTH), BF),
+        jax.ShapeDtypeStruct((3, KW, WIDTH), F32),
+        jax.ShapeDtypeStruct((WIDTH, DH), F32),
+    )
+    results = pl.pallas_call(
         kernel,
-        out_shape=(
-            jax.ShapeDtypeStruct((ROWS, WIDTH), BF),
-            jax.ShapeDtypeStruct((3, ROWS, WIDTH), BF),
-            jax.ShapeDtypeStruct((3, KW, WIDTH), F32),
-            jax.ShapeDtypeStruct((WIDTH, DH), F32),
-        ),
+        out_shape=[pltpu.VMEM(shape.shape, shape.dtype) for shape in shapes],
         in_specs=[pl.BlockSpec(memory_space=pltpu.SMEM), outside, vmem, outside, outside],
-        out_specs=(vmem, vmem, vmem, vmem),
+        out_specs=[vmem] * 4,
         scratch_shapes=scratch,
         compiler_params=pltpu.CompilerParams(
             collective_id=0, has_side_effects=True, vmem_limit_bytes=58 * 2**20
@@ -615,7 +651,15 @@
             flops=8 * 10**9, bytes_accessed=10**7, transcendentals=10**6
         ),
     )(doc_lengths, projected, conv_weight, out_weight, out_grad)
-    return mixed, grad_projected, grad_conv, grad_out_weight
+    return pl.pallas_call(
+        hand_over,
+        out_shape=shapes,
+        in_specs=[outside] * 4,
+        out_specs=(outside,) * 4,
+        scratch_shapes=[pltpu.SemaphoreType.DMA((4,))],
+        compiler_params=pltpu.CompilerParams(vmem_limit_bytes=2**20),
+        cost_estimate=pl.CostEstimate(flops=0, bytes_accessed=5 * 10**6, transcendentals=0),
+    )(*results)
 
 
 def solution(mesh):

time: 106 us -> 87.9 us (0.83); the launches traced: 106 us -> 86.7 us
  Pallas kernels: 99.7 us -> 86 us
  local copies, waits for them, and re-layouts: 5.88 us -> 0 us
    pallas_call x1 -> x2, Pallas kernels: 99.7 us -> 86 us  [the longest x1 84.6 us: body(): pl.pallas_call(kernel, out_shape=[pltpu.VMEM(shape.shape, shape.dtype) fo...]
    unnamed x8 -> x0, local copies, waits for them, and re-layouts: 5.88 us -> none
where the time goes in v3:
time: 87.9 us; the launch traced here: 86.7 us
  Pallas kernels  86 us (98%)
    pallas_call x1, Pallas kernels, body(): pl.pallas_call(kernel, out_shape=[pltpu.VMEM(shape.shape, shape.dtype) fo...  84.6 us

profile of v3, /device:TPU:6, one launch (start us, length us, event | category | flops | bytes accessed | tf_op | source)
XLA Modules:
  0.0 86.7 jit_solution(17395577733530655569)
XLA Ops:
  0.6 84.6 %shard_map.84 = (bf16[512,512]{1,0:T(8,128)(2,1)S(1)}, bf16[3,512,512]{2,1,0:T(8,128)(2,1)S(1)}, f32[3,4,512]{2,1,0:T(4,128)S(1)}, f32[512,128]{1,0:T(8,128)S(1)}) custom-call(s32[8]{0:T(128)} %docs.1, bf16[3,512,512]{2,1,0:T(8,128)(2,1)} %proj_hbm.1, f32[3,4,512]{2,1,0:T(4,128)} %taps.1, bf16[512,4096]{1,0:T(8,128)(2,1)} %weight_hbm.1, ...), custom_call_target="tpu_custom_call" | custom-call | flops 8000000000 | bytes 10000000 | tf_op jit(solution)/shard_map/pallas_call | solution.py:641
  85.2 1.4 %shard_map.85 = (bf16[512,512]{1,0:T(8,128)(2,1)}, bf16[3,512,512]{2,1,0:T(8,128)(2,1)}, f32[3,4,512]{2,1,0:T(4,128)}, f32[512,128]{1,0:T(8,128)}) custom-call(bf16[512,512]{1,0:T(8,128)(2,1)S(1)} %get-tuple-element.8.refs_0_, bf16[3,512,512]{2,1,0:T(8,128)(2,1)S(1)} %get-tuple-element.9.refs_1_, f32[3,4,512]{2,1,0:T(4,128)S(1)} %get-tuple-element.10.refs_2_, ...), custom_call_target="tpu_custom_call" | custom-call | bytes 5000000 | tf_op jit(solution)/shard_map/pallas_call | solution.py:654

commit v4 on v3

--- a/solution.py
+++ b/solution.py
@@ -230,7 +230,7 @@
             activate(stream, acc, slice(None), lanes)
         return 0
 
-    lax.fori_loop(0, HEADS, convolve, 0)
+    lax.fori_loop(0, HEADS, convolve, 0, unroll=True)
     rim_copy.wait_recv()
 
     def convolve_rim(number, _):
@@ -246,7 +246,7 @@
             activate(stream, acc, slice(0, EDGE), lanes)
         return 0
 
-    lax.fori_loop(0, HEADS, convolve_rim, 0)
+    lax.fori_loop(0, HEADS, convolve_rim, 0, unroll=True)
 
     def tail_state(number, _):
         lanes = lanes_of(number)
@@ -261,7 +261,7 @@
             for k in range(1, NZ)
         ]
 
-    lax.fori_loop(0, HEADS, tail_state, 0)
+    lax.fori_loop(0, HEADS, tail_state, 0, unroll=True)
     fwd_copies = to_owners(fwd_send, fwd_in)
     fwd_in[z] = fwd_send[z]
 
@@ -280,7 +280,7 @@
             unit[rows, lanes] = dot(kept, val[0:width, lanes])
         return 0
 
-    lax.fori_loop(0, HEADS, local_attention, 0)
+    lax.fori_loop(0, HEADS, local_attention, 0, unroll=True)
 
     for copy in fwd_copies:
         copy.wait_recv()
@@ -304,7 +304,7 @@
             gunit[rows, :] = part if first else gunit[rows, :] + part
             return 0
 
-        lax.fori_loop(0, ROWS // 256, tile, 0)
+        lax.fori_loop(0, ROWS // 256, tile, 0, unroll=True)
 
     add_gunit(block_of(y), True)
     row_copy.wait_recv()
@@ -321,8 +321,6 @@
     sib_down = links.start(whole(down), whole(down), sibling)
     down_top.wait_recv()
     sib_up = links.start(whole(up), whole(up), sibling)
-    add_gunit(block_of(down))
-    add_gunit(block_of(up))
 
     for copy in out_copies:
         copy.wait_recv()
@@ -339,7 +337,7 @@
         normed_t[lanes_of(number), :] = scaled.T.astype(BF)
         return 0
 
-    lax.fori_loop(0, HEADS, finish_attention, 0)
+    lax.fori_loop(0, HEADS, finish_attention, 0, unroll=True)
 
     def weight_band(band):
         def one_block(which, _):
@@ -353,7 +351,7 @@
                 gz[band, which * 4 + j] = tile.reshape(2, ZROWS // 2, DH)
             return 0
 
-        lax.fori_loop(0, 2, one_block, 0)
+        lax.fori_loop(0, 2, one_block, 0, unroll=True)
 
     ring_x = Ring(links, NX, x, at_x, lambda to: gx.at[pl.ds(to * NZ, NZ)], gx_half, gx_block)
     order = [y, down, up, across]
@@ -363,17 +361,19 @@
     ]
     weight_band(y)
     rings_z[0].begin()
+    add_gunit(block_of(down))
+    add_gunit(block_of(up))
     sib_down.wait_recv()
-    add_gunit(other(down))
-    sib_up.wait_recv()
-    add_gunit(other(up))
+    weight_band(down)
+    rings_z[1].begin()
     pass_top.wait_recv()
     pass_bottom.wait_recv()
     sib_across = links.start(whole(across), whole(across), sibling)
-    weight_band(down)
-    rings_z[1].begin()
+    sib_up.wait_recv()
     weight_band(up)
     rings_z[2].begin()
+    add_gunit(other(down))
+    add_gunit(other(up))
     add_gunit(block_of(across))
     sib_across.wait_recv()
     add_gunit(other(across))
@@ -392,7 +392,7 @@
         bwd_send[pl.ds(2 * number, 2)] = local.astype(BF).reshape(2, DH // 2, DH)
         return 0
 
-    lax.fori_loop(0, HEADS, grad_attn, 0)
+    lax.fori_loop(0, HEADS, grad_attn, 0, unroll=True)
     bwd_copies = to_owners(bwd_send, bwd_in)
     bwd_in[z] = bwd_send[z]
     rings_z[0].relay(2)
@@ -408,7 +408,7 @@
             put(r, dot(normed[rows, :], weight[:, columns]))
             return 0
 
-        lax.fori_loop(0, 2, tile, 0)
+        lax.fori_loop(0, 2, tile, 0, unroll=True)
 
     sib_copies = []
     for k, to in enumerate(outward + [y]):
@@ -471,7 +471,7 @@
     gout_copies = to_owners(bwd_out, gstate)
     gstate[z] = bwd_out[z]
 
-    lax.fori_loop(0, HEADS, backward_local, 0)
+    lax.fori_loop(0, HEADS, backward_local, 0, unroll=True)
     rings_z[3].relay(3)
     rings_z[1].relay(4)
     rings_z[2].relay(4)
@@ -495,7 +495,7 @@
         gacts[2, :, lanes] = gacts[2, :, lanes] + back
         return 0
 
-    lax.fori_loop(0, HEADS, backward_state, 0)
+    lax.fori_loop(0, HEADS, backward_state, 0, unroll=True)
     grim_copy = links.start(gacts.at[:, pl.ds(0, 8)], grim, token_prev)
     ring_y.relay(2)
     rings_z[3].relay(4)
@@ -521,12 +521,29 @@
         return 0
 
     tap_part[12:16, :] = jnp.zeros((4, WIDTH), F32)
-    lax.fori_loop(0, HEADS, unconvolve, 0)
+    lax.fori_loop(0, 2, unconvolve, 0, unroll=True)
+
+    ring_x2 = Ring(links, NZ, z, at_z, lambda to: gx2.at[to], gx2_half, gx2_block)
+    ring_z2 = Ring(links, NX, x, at_x, lambda to: gz2.at[to], gz2_half, gz2_block)
+    own, first, last = ring_x.finish()
+    for k in range(NZ):
+        value = own[k].astype(F32) + first[k].astype(F32) + last[k].astype(F32)
+        gx2[k] = value.astype(BF).reshape(2, XROWS // 2, DH)
+    ring_x2.begin()
+    lax.fori_loop(2, HEADS, unconvolve, 0, unroll=True)
     tap_send[...] = tap_part[...].astype(BF)
     tap_copies = [
         links.start(tap_send, tap_in.at[z], at_z(wrap(z + k, NZ))) for k in range(1, NZ)
     ]
     tap_in[z] = tap_send[...]
+
+    ring_x2.relay(2)
+    for ring, band in zip(rings_z, order):
+        own, first, last = ring.finish()
+        for r in range(2):
+            value = own[r].astype(F32) + first[r].astype(F32) + last[r].astype(F32)
+            gz2[band, r] = value.astype(BF)
+    ring_z2.begin()
 
     grim_copy.wait_recv()
 
@@ -544,22 +561,9 @@
             gproj_out[stream, ROWS - EDGE : ROWS, lanes] = acc.astype(BF)
         return 0
 
-    lax.fori_loop(0, HEADS, unconvolve_rim, 0)
-
-    ring_x2 = Ring(links, NZ, z, at_z, lambda to: gx2.at[to], gx2_half, gx2_block)
-    ring_z2 = Ring(links, NX, x, at_x, lambda to: gz2.at[to], gz2_half, gz2_block)
-
-    for ring, band in zip(rings_z, order):
-        own, first, last = ring.finish()
-        for r in range(2):
-            value = own[r].astype(F32) + first[r].astype(F32) + last[r].astype(F32)
-            gz2[band, r] = value.astype(BF)
-    ring_z2.begin()
-    own, first, last = ring_x.finish()
-    for k in range(NZ):
-        value = own[k].astype(F32) + first[k].astype(F32) + last[k].astype(F32)
-        gx2[k] = value.astype(BF).reshape(2, XROWS // 2, DH)
-    ring_x2.begin()
+    ring_x2.relay(3)
+    lax.fori_loop(0, HEADS, unconvolve_rim, 0, unroll=True)
+
     ring_z2.relay(2)
 
     for copy in tap_copies:
@@ -572,13 +576,12 @@
         links.start(tap_row, tap_rowin.at[x], at_x(wrap(x + k, NX))) for k in range(1, NX)
     ]
     tap_rowin[x] = tap_row[...]
-    ring_x2.relay(2)
 
     own, first, last = ring_y.finish()
     for r in range(2):
         value = own[r].astype(F32) + first[r].astype(F32) + last[r].astype(F32)
         mixed_out[r * half : (r + 1) * half, :] = value.astype(BF)
-    ring_x2.relay(3)
+    ring_x2.relay(4)
 
     for copy in row_copies:
         copy.wait_recv()
@@ -587,7 +590,6 @@
         summed = summed + tap_rowin[k]
     for stream in range(3):
         gtaps_out[stream] = summed[4 * stream : 4 * stream + 4, :]
-    ring_x2.relay(4)
 
     for ring, base, count in ((ring_z2, XROWS, ZROWS // 2), (ring_x2, 0, XROWS // 2)):
         own, first, last = ring.finish()

time: 87.9 us -> 82.1 us (0.934)
  Pallas kernels: 86 us -> 80 us
    pallas_call x1, Pallas kernels: 84.6 us -> 78.6 us  [body(): pl.pallas_call(kernel, out_shape=[pltpu.VMEM(shape.shape, shape.dtype) fo...]
where the time goes in v4:
time: 82.1 us; the launch traced here: 80.8 us
  Pallas kernels  80 us (97%)
    pallas_call x1, Pallas kernels, body(): pl.pallas_call(kernel, out_shape=[pltpu.VMEM(shape.shape, shape.dtype) fo...  78.6 us

profile of v4, /device:TPU:6, one launch (start us, length us, event | category | flops | bytes accessed | tf_op | source)
XLA Modules:
  0.0 80.8 jit_solution(13704905858639569217)
XLA Ops:
  0.6 78.6 %shard_map.84 = (bf16[512,512]{1,0:T(8,128)(2,1)S(1)}, bf16[3,512,512]{2,1,0:T(8,128)(2,1)S(1)}, f32[3,4,512]{2,1,0:T(4,128)S(1)}, f32[512,128]{1,0:T(8,128)S(1)}) custom-call(s32[8]{0:T(128)} %docs.1, bf16[3,512,512]{2,1,0:T(8,128)(2,1)} %proj_hbm.1, f32[3,4,512]{2,1,0:T(4,128)} %taps.1, bf16[512,4096]{1,0:T(8,128)(2,1)} %weight_hbm.1, ...), custom_call_target="tpu_custom_call" | custom-call | flops 8000000000 | bytes 10000000 | tf_op jit(solution)/shard_map/pallas_call | solution.py:643
  79.2 1.4 %shard_map.85 = (bf16[512,512]{1,0:T(8,128)(2,1)}, bf16[3,512,512]{2,1,0:T(8,128)(2,1)}, f32[3,4,512]{2,1,0:T(4,128)}, f32[512,128]{1,0:T(8,128)}) custom-call(bf16[512,512]{1,0:T(8,128)(2,1)S(1)} %get-tuple-element.8.refs_0_, bf16[3,512,512]{2,1,0:T(8,128)(2,1)S(1)} %get-tuple-element.9.refs_1_, f32[3,4,512]{2,1,0:T(4,128)S(1)} %get-tuple-element.10.refs_2_, ...), custom_call_target="tpu_custom_call" | custom-call | bytes 5000000 | tf_op jit(solution)/shard_map/pallas_call | solution.py:656

commit v5 on v4

--- a/solution.py
+++ b/solution.py
@@ -18,7 +18,7 @@
 F32 = jnp.float32
 MESH = pl.DeviceIdType.MESH
 COPIES = 144
-ZROWS = 256
+ZROWS = 320
 XROWS = WIDTH - ZROWS
 
 

time: 82.1 us -> 83.4 us (1.016)
  Pallas kernels: 80 us -> 81.5 us
    pallas_call x1, Pallas kernels: 78.6 us -> 80 us  [body(): pl.pallas_call(kernel, out_shape=[pltpu.VMEM(shape.shape, shape.dtype) fo...]
where the time goes in v5:
time: 83.4 us; the launch traced here: 82.3 us
  Pallas kernels  81.5 us (98%)
    pallas_call x1, Pallas kernels, body(): pl.pallas_call(kernel, out_shape=[pltpu.VMEM(shape.shape, shape.dtype) fo...  80 us

profile of v5, /device:TPU:6, one launch (start us, length us, event | category | flops | bytes accessed | tf_op | source)
XLA Modules:
  0.0 82.3 jit_solution(7688358609781676272)
XLA Ops:
  0.6 80.0 %shard_map.84 = (bf16[512,512]{1,0:T(8,128)(2,1)S(1)}, bf16[3,512,512]{2,1,0:T(8,128)(2,1)S(1)}, f32[3,4,512]{2,1,0:T(4,128)S(1)}, f32[512,128]{1,0:T(8,128)S(1)}) custom-call(s32[8]{0:T(128)} %docs.1, bf16[3,512,512]{2,1,0:T(8,128)(2,1)} %proj_hbm.1, f32[3,4,512]{2,1,0:T(4,128)} %taps.1, bf16[512,4096]{1,0:T(8,128)(2,1)} %weight_hbm.1, ...), custom_call_target="tpu_custom_call" | custom-call | flops 8000000000 | bytes 10000000 | tf_op jit(solution)/shard_map/pallas_call | solution.py:643
  80.7 1.4 %shard_map.85 = (bf16[512,512]{1,0:T(8,128)(2,1)}, bf16[3,512,512]{2,1,0:T(8,128)(2,1)}, f32[3,4,512]{2,1,0:T(4,128)}, f32[512,128]{1,0:T(8,128)}) custom-call(bf16[512,512]{1,0:T(8,128)(2,1)S(1)} %get-tuple-element.8.refs_0_, bf16[3,512,512]{2,1,0:T(8,128)(2,1)S(1)} %get-tuple-element.9.refs_1_, f32[3,4,512]{2,1,0:T(4,128)S(1)} %get-tuple-element.10.refs_2_, ...), custom_call_target="tpu_custom_call" | custom-call | bytes 5000000 | tf_op jit(solution)/shard_map/pallas_call | solution.py:656

commit v6 on v4

--- a/solution.py
+++ b/solution.py
@@ -427,6 +427,9 @@
 
         project(block_of(to), put)
 
+    for k, to in enumerate(outward):
+        put_own(k, to)
+    ring_y.begin()
     rings_z[1].relay(2)
     rings_z[2].relay(2)
     rings_z[0].relay(3)
@@ -440,10 +443,8 @@
         run = bwd_in[k].astype(F32) + same(k, k + 1) * run
     bwd_row[...] = run.astype(BF)
     back_copy = links.start(bwd_row, bwd_rowin, at_x(wrap(x - 1, NX)))
-
-    for k, to in enumerate(outward):
-        put_own(k, to)
-    ring_y.begin()
+    put_own(3, y)
+
     rings_z[3].relay(2)
     rings_z[1].relay(3)
     rings_z[2].relay(3)
@@ -475,7 +476,6 @@
     rings_z[3].relay(3)
     rings_z[1].relay(4)
     rings_z[2].relay(4)
-    put_own(3, y)
 
     for copy in gout_copies:
         copy.wait_recv()

time: 82.1 us -> 80.8 us (0.984); the launches traced: 80.8 us -> 80.6 us
  no operation moved by 1% of the time
where the time goes in v6:
time: 80.8 us; the launch traced here: 80.6 us
  Pallas kernels  79.8 us (99%)
    pallas_call x1, Pallas kernels, body(): pl.pallas_call(kernel, out_shape=[pltpu.VMEM(shape.shape, shape.dtype) fo...  78.4 us

profile of v6, /device:TPU:6, one launch (start us, length us, event | category | flops | bytes accessed | tf_op | source)
XLA Modules:
  0.0 80.6 jit_solution(11231609292966002363)
XLA Ops:
  0.6 78.4 %shard_map.84 = (bf16[512,512]{1,0:T(8,128)(2,1)S(1)}, bf16[3,512,512]{2,1,0:T(8,128)(2,1)S(1)}, f32[3,4,512]{2,1,0:T(4,128)S(1)}, f32[512,128]{1,0:T(8,128)S(1)}) custom-call(s32[8]{0:T(128)} %docs.1, bf16[3,512,512]{2,1,0:T(8,128)(2,1)} %proj_hbm.1, f32[3,4,512]{2,1,0:T(4,128)} %taps.1, bf16[512,4096]{1,0:T(8,128)(2,1)} %weight_hbm.1, ...), custom_call_target="tpu_custom_call" | custom-call | flops 8000000000 | bytes 10000000 | tf_op jit(solution)/shard_map/pallas_call | solution.py:643
  79.0 1.4 %shard_map.85 = (bf16[512,512]{1,0:T(8,128)(2,1)}, bf16[3,512,512]{2,1,0:T(8,128)(2,1)}, f32[3,4,512]{2,1,0:T(4,128)}, f32[512,128]{1,0:T(8,128)}) custom-call(bf16[512,512]{1,0:T(8,128)(2,1)S(1)} %get-tuple-element.8.refs_0_, bf16[3,512,512]{2,1,0:T(8,128)(2,1)S(1)} %get-tuple-element.9.refs_1_, f32[3,4,512]{2,1,0:T(4,128)S(1)} %get-tuple-element.10.refs_2_, ...), custom_call_target="tpu_custom_call" | custom-call | bytes 5000000 | tf_op jit(solution)/shard_map/pallas_call | solution.py:656
